TPU v7x, 256 devices: a whole 4x4x8 slice. The times are simulated.
256 devices in a mesh: seq: 32 (over z, x), head: 8 (over y, core).
Axes of the slice: x: 4, y: 4, z: 8, core: 2. Of those that a mesh axis runs over, the one named last changes fastest.
Arguments:
- queries: bfloat16 [6144, 8192], P('seq', 'head'), may hold values from -20 to 20
- image_kv: bfloat16 [64, 256, 2, 1024], P('seq', 'head'), may hold values from -6 to 6
- gate_logit: float32 [64], P('head'), may hold values from 0.3 to 1.5
- d_gated: bfloat16 [6144, 8192], P('seq', 'head'), may hold values from -6 to 6
- media_list: int32 [32, 16], replicated, may hold values from 0 to 63, as said below
- media_count: int32 [32], replicated, may hold values from 12 to 16, as said below
- image_slot: int32 [64], replicated, may hold values from 0 to 63, as said below
Outputs:
- gated: bfloat16 [6144, 8192], P('seq', 'head')
- d_queries: bfloat16 [6144, 8192], P('seq', 'head')
- d_image_kv: bfloat16 [64, 256, 2, 1024], P('seq', 'head')
Inputs may be any that keep to these rules, and one draw needn't show every extreme that they name: `media_list`: the 16 images of one segment's list lie in slots of 16 different owners (image_slot // 2 differ); ids in a row are distinct. `media_count`: the last segment attends its whole list. `image_slot`: A permutation of the slots.
All inputs are finite; a program needn't handle non-finite values.
Results may differ from a plain program's by a relative error of at most 0.022.
Values may be sent and summed in bfloat16 or wider, within the bound.
A program may use at most 128 MiB of HBM per device.

v0:
```python
import jax
import jax.numpy as jnp
from jax import lax
from jax.sharding import PartitionSpec as P

HD = 128


def attend_scores(query_rows, key_rows, inv_root):
    return (
        jnp.einsum("tgd,vd->tgv", query_rows, key_rows, preferred_element_type=jnp.float32)
        * inv_root
    )


def on_device(queries, image_kv, gate_logit, d_gated, media_list, media_count, image_slot):
    my_index = lax.axis_index("seq")
    seq_count = lax.axis_size("seq")
    per_owner = image_kv.shape[0]
    tok_rows = queries.shape[0]
    group_size = queries.shape[1] // HD
    inv_root = HD ** (-0.5)
    query_rows = queries.reshape(tok_rows, group_size, HD)
    my_list = media_list[my_index]
    live_count = media_count[my_index]
    my_slots = jnp.take(image_slot, my_list)
    media_slots = my_slots.shape[0]
    slot_ids = jnp.arange(media_slots)
    live_mask = slot_ids < live_count
    by_head = lax.all_to_all(image_kv, "head", split_axis=3, concat_axis=1, tiled=True)
    block_rows = lax.all_gather(by_head, "seq", axis=0, tiled=True)
    row_ids = jnp.arange(block_rows.shape[0])
    one_hot = (my_slots[:, None] == row_ids[None, :]).astype(jnp.bfloat16)
    chosen = jnp.einsum(
        "mr,rvkd->mvkd", one_hot, block_rows, preferred_element_type=jnp.float32
    ).astype(jnp.bfloat16)
    key_stack = chosen[:, :, 0, :]
    value_stack = chosen[:, :, 1, :]
    image_tokens = chosen.shape[1]

    def top_step(slot_index, state):
        top_now, total_now = state
        key_rows = lax.dynamic_index_in_dim(key_stack, slot_index, 0, keepdims=False)
        scores = attend_scores(query_rows, key_rows, inv_root)
        top_next = jnp.maximum(top_now, jnp.max(scores, axis=-1))
        total_next = total_now * jnp.exp(top_now - top_next) + jnp.sum(
            jnp.exp(scores - top_next[..., None]), axis=-1
        )
        return (top_next, total_next)

    top_init = jnp.full((tok_rows, group_size), -jnp.inf, jnp.float32)
    total_init = jnp.zeros((tok_rows, group_size), jnp.float32)
    row_top, row_total = lax.fori_loop(0, live_count, top_step, (top_init, total_init))

    def probs_of(slot_index):
        key_rows = lax.dynamic_index_in_dim(key_stack, slot_index, 0, keepdims=False)
        scores = attend_scores(query_rows, key_rows, inv_root)
        return jnp.exp(scores - row_top[..., None]) / row_total[..., None]

    def value_step(slot_index, running):
        probs_low = probs_of(slot_index).astype(jnp.bfloat16)
        value_rows = lax.dynamic_index_in_dim(value_stack, slot_index, 0, keepdims=False)
        return running + jnp.einsum(
            "tgv,vd->tgd", probs_low, value_rows, preferred_element_type=jnp.float32
        )

    attended = lax.fori_loop(
        0, live_count, value_step, jnp.zeros((tok_rows, group_size, HD), jnp.float32)
    )
    gate_tanh = jnp.tanh(gate_logit)[None, :, None]
    gated = (gate_tanh * attended).astype(jnp.bfloat16).reshape(tok_rows, group_size * HD)
    d_attended = (gate_tanh * d_gated.reshape(tok_rows, group_size, HD).astype(jnp.float32)).astype(
        jnp.bfloat16
    )
    row_delta = jnp.sum(d_attended.astype(jnp.float32) * attended, axis=-1)

    def grad_step(slot_index, state):
        query_grad, grad_stack = state
        key_rows = lax.dynamic_index_in_dim(key_stack, slot_index, 0, keepdims=False)
        value_rows = lax.dynamic_index_in_dim(value_stack, slot_index, 0, keepdims=False)
        probs = probs_of(slot_index)
        probs_low = probs.astype(jnp.bfloat16)
        d_probs = jnp.einsum(
            "tgd,vd->tgv", d_attended, value_rows, preferred_element_type=jnp.float32
        )
        d_scores = (probs * (d_probs - row_delta[..., None])).astype(jnp.bfloat16)
        query_grad = query_grad + jnp.einsum(
            "tgv,vd->tgd", d_scores, key_rows, preferred_element_type=jnp.float32
        )
        d_keys = (
            jnp.einsum("tgv,tgd->vd", d_scores, query_rows, preferred_element_type=jnp.float32)
            * inv_root
        )
        d_values = jnp.einsum(
            "tgv,tgd->vd", probs_low, d_attended, preferred_element_type=jnp.float32
        )
        both_grads = jnp.stack([d_keys, d_values], axis=1).astype(jnp.bfloat16)
        grad_stack = lax.dynamic_update_index_in_dim(grad_stack, both_grads, slot_index, 0)
        return (query_grad, grad_stack)

    grad_init = jnp.zeros((media_slots, image_tokens, 2, HD), jnp.bfloat16)
    query_grad, grad_stack = lax.fori_loop(
        0, live_count, grad_step, (jnp.zeros((tok_rows, group_size, HD), jnp.float32), grad_init)
    )
    d_queries = (query_grad * inv_root).astype(jnp.bfloat16).reshape(tok_rows, group_size * HD)
    image_ids = jnp.arange(seq_count * per_owner)
    placing = ((my_slots[:, None] == image_ids[None, :]) & live_mask[:, None]).astype(jnp.bfloat16)
    full_grad = jnp.einsum("mi,mvkd->ivkd", placing, grad_stack, preferred_element_type=jnp.float32)
    summed = lax.psum_scatter(
        full_grad.astype(jnp.bfloat16), "seq", scatter_dimension=0, tiled=True
    )
    d_image_kv = lax.all_to_all(summed, "head", split_axis=1, concat_axis=3, tiled=True)
    return (gated, d_queries, d_image_kv)


def solution(mesh):
    return jax.shard_map(
        on_device,
        mesh=mesh,
        in_specs=(
            P("seq", "head"),
            P("seq", "head", None, None),
            P("head"),
            P("seq", "head"),
            P(),
            P(),
            P(),
        ),
        out_specs=(P("seq", "head"), P("seq", "head"), P("seq", "head", None, None)),
        check_vma=False,
    )
```

profile of v0, /device:TPU:1, one launch (start us, length us, event | category | flops | bytes accessed | tf_op | source)
XLA Modules:
  0.0 553.0 jit_solution(13628894717123313889)
XLA Ops:
  7.2 2.4 copy.58
  10.6 12.3 %all_to_all.36 = bf16[8,2,8192]{2,1,0:T(2,128)(2,1)S(1)} all-to-all(bf16[8,2,8192]{2,1,0:T(2,128)(2,1)S(1)} %reshape.132), channel_id=1, replica_groups=mesh['seq'=32,'head'=8] {'head'}, dimensions={0} | all-to-all | bytes 524288 | tf_op jit(solution)/shard_map/all_to_all | solution.py:30
  23.4 2.3 copy.59
  28.8 96.3 %all-gather.2.cloned.1.call-done = bf16[64,256,2,128]{3,1,2,0:T(8,128)(2,1)} async-done(((bf16[2,256,2,128]{3,1,2,0:T(8,128)(2,1)}), bf16[64,256,2,128]{3,1,2,0:T(8,128)(2,1)}) %all-gather.2.cloned.1.call-update) | async-done | bytes 8388624 | tf_op jit(solution)/shard_map/all_gather | solution.py:31
  125.1 10.3 %fusion.39 = bf16[16,256,2,128]{3,0,2,1:T(8,128)(2,1)S(1)} fusion(bf16[64,256,2,128]{3,1,2,0:T(8,128)(2,1)} %all-gather.2.cloned.1.call-done, s32[16]{0:T(128)S(1)} %and_select_fusion), kind=kOutput, calls=%fused_computation.50 | convolution fusion | flops 135267328 | bytes 10485824 | tf_op jit(solution)/shard_map/mr,rvkd->mvkd/dot_general | solution.py:34
  135.7 1.2 copy.66
  137.2 28.7 %while.34 = (s32[]{:T(128)}, f32[192,8]{0,1:T(8,128)S(1)}, f32[192,8]{0,1:T(8,128)S(1)}, s32[]{:T(128)}, bf16[16,256,128]{2,1,0:T(8,128)(2,1)S(1)}, /*index=5*/b...) while((s32[]{:T(128)}, f32[192,8]{0,1:T(8,128)S(1)}, f32[192,8]{0,1:T(8,128)S(1)}, s32[]{:T(128)}, ...), condition=%wide.region_3.4_spmd, body=%wide.region_0.3_spmd.sunk | while | flops 102239232 | bytes 3684491 | solution.py:53
  166.9 38.7 %while.35 = (s32[]{:T(128)}, f32[192,8,128]{2,1,0:T(8,128)S(1)}, s32[]{:T(128)}, bf16[16,256,128]{2,1,0:T(8,128)(2,1)S(1)}, bf16[192,8,128]{2,1,0:T(8,128)(2,1)S...) while((s32[]{:T(128)}, f32[192,8,128]{2,1,0:T(8,128)S(1)}, ...), condition=%wide.region_5.6_spmd, body=%wide.region_4.5_spmd.sunk | while | flops 203096064 | bytes 2294935 | solution.py:67
  167.5 1.9 convolution_add_fusion.4
  170.1 1.9 convolution_add_fusion.4
  172.6 1.9 convolution_add_fusion.4
  175.1 1.9 convolution_add_fusion.4
  177.7 1.9 convolution_add_fusion.4
  180.2 1.9 convolution_add_fusion.4
  182.8 1.9 convolution_add_fusion.4
  185.3 1.9 convolution_add_fusion.4
  187.8 1.9 convolution_add_fusion.4
  190.4 1.9 convolution_add_fusion.4
  192.9 1.9 convolution_add_fusion.4
  195.4 1.9 convolution_add_fusion.4
  198.0 1.9 convolution_add_fusion.4
  200.5 1.9 convolution_add_fusion.4
  203.1 1.9 convolution_add_fusion.4
  206.0 1.8 broadcast_in_dim.14
  207.9 68.9 %while.36 = (s32[]{:T(128)}, f32[192,8,128]{2,1,0:T(8,128)S(1)}, bf16[16,256,2,128]{3,1,2,0:T(8,128)(2,1)}, s32[]{:T(128)}, bf16[16,256,128]{2,1,0:T(8,128)(2,1)...) while((s32[]{:T(128)}, f32[192,8,128]{2,1,0:T(8,128)S(1)}, ...), condition=%wide.region_8.9_spmd, body=%wide.region_7.8_spmd.sunk | while | flops 506626048 | bytes 10836159 | solution.py:102
  232.2 1.2 fusion.93
  276.8 7.3 %convolution_convert_fusion = bf16[64,256,2,128]{3,0,2,1:T(8,128)(2,1)} fusion(bf16[16,256,2,128]{3,1,2,0:T(8,128)(2,1)} %get-tuple-element.143, s32[16]{0:T(128)S(1)} %and_select_fusion, pred[16]{0:T(512)(128)(4,1)S(1)} %iota_compare_fusion.1), kind=kOutput, calls=%fused_computation.48 | convolution fusion | flops 138414080 | bytes 10485840 | tf_op jit(solution)/shard_map/mi,mvkd->ivkd/dot_general | solution.py:108
  284.1 12.0 %copy.73 = bf16[64,256,2,128]{3,1,2,0:T(8,128)(2,1)} copy(bf16[64,256,2,128]{3,0,2,1:T(8,128)(2,1)} %convolution_convert_fusion) | data formatting | bytes 16777216 | tf_op jit(solution)/shard_map/convert_element_type | solution.py:110
  296.2 231.6 %reduce-scatter.2.cloned.1.call-done = bf16[2,256,2,128]{3,1,2,0:T(8,128)(2,1)} async-done(((bf16[64,256,2,128]{3,1,2,0:T(8,128)(2,1)}), bf16[2,256,2,128]{3,1,2,0:T(8,128)(2,1)}) %reduce-scatter.2.cloned.1.call-update) | async-done | bytes 262160 | tf_op jit(solution)/shard_map/reduce_scatter | solution.py:109
  527.7 1.9 copy.74
  529.7 8.9 %all-to-all-start.1 = ((bf16[2,256,2,128]{3,2,0,1:T(2,128)(2,1)}), bf16[2,256,2,128]{3,2,0,1:T(2,128)(2,1)S(1)}, u32[]{:S(2)}, u32[]{:S(2)}) async-start(bf16[2,256,2,128]{3,2,0,1:T(2,128)(2,1)} %copy.74), calls=%async_computation.2 | async-start | bytes 524288 | tf_op jit(solution)/shard_map/all_to_all | solution.py:112
  539.6 5.5 all-to-all-done.1
  (210 shorter events, 82.8 us)
Async XLA Ops:
  7.2 20.0 %copy-start = (s32[32,16]{0,1:T(8,128)S(1)}, s32[32,16]{0,1:T(8,128)}, u32[]{:S(2)}) copy-start(s32[32,16]{0,1:T(8,128)} %param.17) | copy-start | bytes 6148
  7.2 117.9 %all-gather.2.cloned.1.call-start = ((), (), s32[]{:S(2)}) async-start(), calls=%async_computation.3 | async-start | bytes 8650752 | tf_op jit(solution)/shard_map/all_gather | solution.py:31
  22.9 2.9 copy-start.4
  22.9 2.9 copy-start.2
  22.9 3.0 copy-start.3
  25.7 502.0 %reduce-scatter.2.cloned.1.call-start = ((), (), s32[]{:S(2)}) async-start(), calls=%async_computation.4 | async-start | bytes 8650752 | tf_op jit(solution)/shard_map/reduce_scatter | solution.py:109
  26.0 0.7 copy-start.5
  26.0 1.4 copy-start.1
  529.7 15.4 %all-to-all-start.1 = ((bf16[2,256,2,128]{3,2,0,1:T(2,128)(2,1)}), bf16[2,256,2,128]{3,2,0,1:T(2,128)(2,1)S(1)}, u32[]{:S(2)}, u32[]{:S(2)}) async-start(bf16[2,256,2,128]{3,2,0,1:T(2,128)(2,1)} %copy.74), calls=%async_computation.2 | async-start | bytes 524288 | tf_op jit(solution)/shard_map/all_to_all | solution.py:112
Sparse Core Ops, SparseCore 0:
  25.8 99.2 all-gather.1
  296.2 231.4 reduce-scatter.1
where the time goes:
time: 555 us; the launch traced here: 553 us
  waiting for transfers between devices  333 us (60%)
  matrix products  101 us (18%)
  loops' own time  32.9 us (6%)
  local copies, waits for them, and re-layouts  29 us (5%)
  other arithmetic  20.6 us (4%)
  between operations  14.3 us (3%)
  blocking collectives  12.3 us (2%)
  starting transfers between devices  8.99 us (2%)
    reduce_scatter x1, waiting for transfers between devices, on_device(): lax.psum_scatter(full_grad.astype(jnp.bfloat16), 'seq', scatter_dimension...  232 us
    all_gather x1, waiting for transfers between devices, on_device(): block_rows = lax.all_gather(by_head, 'seq', axis=0, tiled=True)  96.3 us
    dot_general x15, matrix products, value_step(): jnp.einsum('tgv,vd->tgd', probs_low, value_rows, preferred_element_type=j...  28 us
    dot_general x15, matrix products, grad_step(): jnp.einsum('tgd,vd->tgv', d_attended, value_rows, preferred_element_type=...  18.4 us
    dot_general x30, matrix products, attend_scores(): jnp.einsum('tgd,vd->tgv', query_rows, key_rows, preferred_element_type=jn...  16.4 us
    all_to_all x1, blocking collectives, on_device(): lax.all_to_all(image_kv, 'head', split_axis=3, concat_axis=1, tiled=True)  12.3 us
    convert_element_type x1, local copies, waits for them, and re-layouts, on_device(): full_grad.astype(jnp.bfloat16)  12 us
    another operation x1, loops' own time, on_device(): lax.fori_loop(0, live_count, top_step, (top_init, total_init))  11.1 us
  transfers between devices with their start and end apart: 3, of which 3 were waited for; matrix products, arithmetic and copies ran while one was open for 1% of the time, Pallas kernels for 0%

commit v1 on v0

v1 whole, which is shorter than its diff:
```python
import functools

import jax
import jax.numpy as jnp
from jax import lax
from jax.experimental import pallas as pl
from jax.experimental.pallas import tpu as pltpu
from jax.sharding import PartitionSpec as P

MESH = pl.DeviceIdType.MESH
HD = 128
XN = 4
ZN = 8
HN = 8
MEDIA = 16
LOWEST = 12
TOK = 192
ROWS = 1536
HALF = 768
RB = 256
KEYS = 1024
PART = 64
SLOTS = 64
LOG2E = 1.4426950408889634
INV_ROOT = HD ** (-0.5)
F32 = jnp.float32
BF16 = jnp.bfloat16


def mod(value, n):
    return lax.rem(value + n, n)


def nt_dot(a, b):
    return lax.dot_general(a, b, (((1,), (1,)), ((), ())), preferred_element_type=F32)


def nn_dot(a, b):
    return jnp.dot(a, b, preferred_element_type=F32)


def kernel(
    slots_ref, counts_ref, inv_ref, gate_ref, q_ref, dg_ref, kv_ref,
    gated_ref, dq_ref, dkv_ref,
    kall, vall, qall, daall, dat, dap, pmat, kc, kt, vc, vt, sbuf, dsbuf, ot,
    stat, statin, fac, dlt, xo, xin, gk, gv, rout, rin, fin, dkvin,
    a2a_s, a2a_r, ag_s, ag_r, xg_s, xg_r, st_s, st_r, xr_s, xr_r, rs_s, rs_r, fa_s, fa_r,
):
    seq = lax.axis_index("seq")
    h = lax.axis_index("head")
    z = seq // XN
    x = lax.rem(seq, XN)
    hq = h // 2
    hp = lax.rem(h, 2)
    kv_all = (kall, vall)
    xg_all = (qall, daall)
    grads = (gk, gv)
    pending = []

    def dev(zz, xx, hh):
        return (zz * XN + xx, hh)

    def send(src, dst, ssem, rsem, device):
        copy = pltpu.make_async_remote_copy(
            src_ref=src, dst_ref=dst, send_sem=ssem, recv_sem=rsem, device_id=device, device_id_type=MESH
        )
        copy.start()
        pending.append(copy)

    def arrived(ref, sem):
        pltpu.make_async_copy(ref, ref, sem).wait()

    z_to = (mod(z + 1, ZN), mod(z - 1, ZN))
    x_to = (mod(x + 1, XN), mod(x - 1, XN))
    x_opp = mod(x + 2, XN)
    self_in = x == hq

    barrier = pltpu.get_barrier_semaphore()

    def greet(device):
        pl.semaphore_signal(barrier, inc=1, device_id=device, device_id_type=MESH)

    for k in range(1, HN):
        greet(dev(z, hq, mod(h + k, HN)))
    for k in range(1, XN):
        greet(dev(z, mod(x + k, XN), 2 * x + hp))
        greet(dev(z, mod(x + k, XN), 2 * x + 1 - hp))
        greet(dev(z, mod(x + k, XN), h))
    greet(dev(z, x, 2 * x + 1 - hp))

    @pl.when(jnp.logical_not(self_in))
    def _():
        greet(dev(z, hq, h))
        greet(dev(z, x, 2 * x + hp))

    for d in range(2):
        greet(dev(z_to[d], x, h))
    pl.semaphore_wait(barrier, jnp.where(self_in, 19, 21))

    def a2a_copy(t, k):
        target = mod(h + k, HN)
        mine = kall if t == 0 else vall
        dst = mine.at[pl.ds(2 * seq, 2), hp]
        return pltpu.make_async_remote_copy(
            src_ref=kv_ref.at[t, target], dst_ref=dst, send_sem=a2a_s.at[t, k],
            recv_sem=a2a_r.at[t, 2 * x + hp], device_id=dev(z, hq, target), device_id_type=MESH,
        )

    for t in range(2):
        for k in range(1, HN):
            a2a_copy(t, k).start()

        @pl.when(jnp.logical_not(self_in))
        def _():
            a2a_copy(t, 0).start()

        @pl.when(self_in)
        def _():
            pltpu.make_async_copy(
                kv_ref.at[t, h], kv_all[t].at[pl.ds(2 * seq, 2), hp], a2a_r.at[t, 2 * x + hp]
            ).start()

    def a2a_wait(t):
        for xx in range(XN):
            for jj in range(2):
                arrived(kv_all[t].at[pl.ds(2 * (z * XN + xx), 2), jj], a2a_r.at[t, 2 * xx + jj])

    def xg_ref(t, c, half):
        return xg_all[t].at[c, half]

    def xg_first(t):
        for pos in range(2):
            for d in range(2):
                half = d if pos == 0 else 1 - d
                ref = xg_ref(t, x, half)
                send(ref, ref, xg_s.at[t, d, pos], xg_r.at[t, d, pos], dev(z, x_to[d], h))

    def xg_wait(t, d, pos):
        c = x_opp if pos == 2 else x_to[1 - d]
        half = 1 - d if pos == 1 else d
        arrived(xg_ref(t, c, half), xg_r.at[t, d, pos])

    def xg_forward(t):
        for d in range(2):
            xg_wait(t, d, 0)
            ref = xg_ref(t, x_to[1 - d], d)
            send(ref, ref, xg_s.at[t, d, 2], xg_r.at[t, d, 2], dev(z, x_to[d], h))

    def ag_ref(t, zz, d, pos):
        sub = d if pos == 0 else 1 - d
        return kv_all[t].at[pl.ds(zz * 8 + 4 * sub, 4)]

    def ag_send(t, k, pos):
        for d in range(2):
            zz = mod(z - (k - 1), ZN) if d == 0 else mod(z + (k - 1), ZN)
            ref = ag_ref(t, zz, d, pos)
            i = 2 * (k - 1) + pos
            send(ref, ref, ag_s.at[t, d, i], ag_r.at[t, d, i], dev(z_to[d], x, h))

    def ag_wait(t, k, pos):
        for d in range(2):
            zz = mod(z - k, ZN) if d == 0 else mod(z + k, ZN)
            arrived(ag_ref(t, zz, d, pos), ag_r.at[t, d, 2 * (k - 1) + pos])

    def ag_step(t, k):
        for pos in range(1 if k == 4 else 2):
            if k > 1:
                ag_wait(t, k - 1, pos)
            ag_send(t, k, pos)

    def ag_end(t):
        ag_wait(t, 3, 1)
        ag_wait(t, 4, 0)

    for g in range(8):
        rows = q_ref[:, g * HD : (g + 1) * HD]
        qall[x, g // 4, (g % 4) * TOK : (g % 4 + 1) * TOK, :] = rows
    xg_first(0)
    for g in range(8):
        rows = dg_ref[:, g * HD : (g + 1) * HD].astype(F32) * gate_ref[g]
        daall[x, g // 4, (g % 4) * TOK : (g % 4 + 1) * TOK, :] = rows.astype(BF16)
    stat[...] = jnp.ones_like(stat)

    a2a_wait(0)
    ag_step(0, 1)
    xg_forward(0)
    xg_first(1)
    ag_step(0, 2)
    a2a_wait(1)
    ag_step(0, 3)
    ag_step(0, 4)
    ag_step(1, 1)
    ag_end(0)

    def pick(src, dst, dst_t, c):
        segment = z * XN + c

        def one(j, carry):
            slot = slots_ref[segment, j]
            dst[c, pl.ds(pl.multiple_of(j * PART, PART), PART), :] = src[slot].reshape(PART, HD)
            return carry

        lax.fori_loop(0, MEDIA, one, 0)
        for ch in range(KEYS // 256):
            block = dst[c, ch * 256 : (ch + 1) * 256, :]
            dst_t[c, :, ch * 256 : (ch + 1) * 256] = block.T

    def lanes(rb):
        return pl.ds(pl.multiple_of(rb * RB, RB), RB)

    def probs_of(c):
        pick(kall, kc, kt, c)
        live = (counts_ref[z * XN + c] - LOWEST) * PART

        def block(rb, carry):
            half = rb // 3
            q_rows = qall[c, half, pl.ds(pl.multiple_of(lax.rem(rb, 3) * RB, RB), RB), :]
            top = None
            for ch in range(4):
                s = nt_dot(kc[c, ch * 256 : (ch + 1) * 256, :], q_rows)
                if ch == 3:
                    row_ids = lax.broadcasted_iota(jnp.int32, (256, RB), 0)
                    s = jnp.where(row_ids < live, s, -1e30)
                sbuf[ch * 256 : (ch + 1) * 256, :] = s
                here = jnp.max(s, axis=0, keepdims=True)
                top = here if top is None else jnp.maximum(top, here)
            total = jnp.zeros((1, RB), F32)
            for ch in range(4):
                p = jnp.exp2((sbuf[ch * 256 : (ch + 1) * 256, :] - top) * (LOG2E * INV_ROOT))
                total = total + jnp.sum(p, axis=0, keepdims=True)
                pmat[c, ch * 256 : (ch + 1) * 256, lanes(rb)] = p.astype(BF16)
            stat[c, 0, pl.ds(rb, 1), :] = top
            stat[c, 1, pl.ds(rb, 1), :] = total
            return carry

        lax.fori_loop(0, 6, block, 0)

    def outs_of(c):
        pick(vall, vc, vt, c)

        def block(rb, carry):
            half = rb // 3
            rows = daall[c, half, pl.ds(pl.multiple_of(lax.rem(rb, 3) * RB, RB), RB), :]
            da_t = rows.T
            dat[c, :, lanes(rb)] = da_t
            o = nn_dot(vt[c], pmat[c, :, lanes(rb)])
            ot[c, :, lanes(rb)] = o
            stat[c, 2, pl.ds(rb, 1), :] = jnp.sum(da_t.astype(F32) * o, axis=0, keepdims=True)
            return carry

        lax.fori_loop(0, 6, block, 0)

    def stat_send(c, i):
        for k in range(1, XN):
            send(
                stat.at[c], statin.at[k - 1, c], st_s.at[i, k - 1], st_r.at[i, k - 1],
                dev(z, mod(x + k, XN), h),
            )

    c_right, c_left = x_to
    probs_of(x)
    ag_step(1, 2)
    xg_wait(0, 0, 1)
    probs_of(c_left)
    xg_forward(1)
    ag_step(1, 3)
    xg_wait(0, 1, 1)
    probs_of(c_right)
    ag_step(1, 4)
    for d in range(2):
        xg_wait(0, d, 2)
    probs_of(x_opp)
    ag_end(1)

    outs_of(x)
    stat_send(x, 0)
    xg_wait(1, 0, 1)
    outs_of(c_left)
    stat_send(c_left, 1)
    xg_wait(1, 1, 1)
    outs_of(c_right)
    stat_send(c_right, 2)
    for d in range(2):
        xg_wait(1, d, 2)
    outs_of(x_opp)
    stat_send(x_opp, 3)
    for i, off in enumerate((0, -1, 1, 2)):
        for k in range(1, XN):
            arrived(statin.at[k - 1, mod(x - k + off + XN, XN)], st_r.at[i, k - 1])

    def combine(c):
        tops = [stat[c, 0]] + [statin[k, c, 0] for k in range(XN - 1)]
        totals = [stat[c, 1]] + [statin[k, c, 1] for k in range(XN - 1)]
        dots = [stat[c, 2]] + [statin[k, c, 2] for k in range(XN - 1)]
        top = functools.reduce(jnp.maximum, tops)
        scales = [jnp.exp2((one - top) * (LOG2E * INV_ROOT)) for one in tops]
        total = sum(a * b for a, b in zip(scales, totals))
        delta = sum(a * b for a, b in zip(scales, dots)) / total
        own = scales[0] / total
        fac[c] = own
        dlt[c] = delta * own

        def block(rb, carry):
            half = rb // 3
            f = fac[c, pl.ds(rb, 1), :]
            cols = pl.ds(pl.multiple_of(lax.rem(rb, 3) * RB, RB), RB)
            xo[0, c, half, :, cols] = (ot[c, :, lanes(rb)] * f).astype(BF16)
            scaled = (dat[c, :, lanes(rb)].astype(F32) * f).astype(BF16)
            dat[c, :, lanes(rb)] = scaled
            dap[c, pl.ds(pl.multiple_of(rb * RB, RB), RB), :] = scaled.T
            return carry

        lax.fori_loop(0, 6, block, 0)

    def xr_opp(t):
        for d in range(2):
            send(xo.at[t, x_opp, d], xin.at[t, d, 0], xr_s.at[t, d, 0], xr_r.at[t, d, 0], dev(z, x_to[d], h))

    def xr_near(t, d):
        send(
            xo.at[t, x_to[d], 1 - d], xin.at[t, d, 1], xr_s.at[t, d, 1], xr_r.at[t, d, 1], dev(z, x_to[d], h)
        )

    def xr_add(t):
        for d in range(2):
            arrived(xin.at[t, d, 0], xr_r.at[t, d, 0])
            both = xo[t, x_to[d], d].astype(F32) + xin[t, d, 0].astype(F32)
            xo[t, x_to[d], d] = both.astype(BF16)
            send(
                xo.at[t, x_to[d], d], xin.at[t, d, 2], xr_s.at[t, d, 2], xr_r.at[t, d, 2], dev(z, x_to[d], h)
            )

    def xr_end(t):
        for d in range(2):
            for i in (1, 2):
                arrived(xin.at[t, d, i], xr_r.at[t, d, i])

    def xr_rows(t, half):
        both = xo[t, x, half].astype(F32) + xin[t, half, 2].astype(F32) + xin[t, 1 - half, 1].astype(F32)
        return both.T

    combine(x_opp)
    xr_opp(0)
    combine(c_right)
    xr_near(0, 0)
    combine(c_left)
    xr_near(0, 1)
    combine(x)

    def value_grads(c):
        for ch in range(2):
            part = nn_dot(pmat[c, ch * 512 : (ch + 1) * 512, :], dap[c])
            gv[c, ch * 8 : (ch + 1) * 8] = part.astype(BF16).reshape(8, PART, HD)

    def over_segments(f):
        def one(c, carry):
            f(c)
            return carry

        lax.fori_loop(0, XN, one, 0)

    over_segments(value_grads)
    xr_add(0)

    def own_part(t, slot):
        out = None
        for c in range(XN):
            entry = inv_ref[z * XN + c, slot]
            block = grads[t][c, jnp.maximum(entry, 0)].astype(F32)
            block = jnp.where(entry >= 0, block, 0.0)
            out = block if out is None else out + block
        return out

    def rs_step(t, i):
        k = (i + 3) // 2
        for d in range(2):
            away = 5 - k
            zt = mod(z + away, ZN) if d == 0 else mod(z - away, ZN)
            sub = d if i % 2 == 0 else 1 - d
            if i >= 2:
                arrived(rin.at[t, d, i - 2], rs_r.at[t, d, i - 2])

            def one(sl, carry):
                part = own_part(t, zt * 8 + 4 * sub + sl)
                if i >= 2:
                    part = part + rin[t, d, i - 2, sl].astype(F32)
                rout[t, d, i, sl] = part.astype(BF16)
                return carry

            lax.fori_loop(0, 4, one, 0)
            send(rout.at[t, d, i], rin.at[t, d, i], rs_s.at[t, d, i], rs_r.at[t, d, i], dev(z_to[d], x, h))

    def rs_end(t):
        for i in (5, 6):
            for d in range(2):
                arrived(rin.at[t, d, i], rs_r.at[t, d, i])
        for sub in range(2):

            def one(sl, carry):
                part = own_part(t, z * 8 + 4 * sub + sl)
                for d in range(2):
                    part = part + rin[t, d, 6 if sub == d else 5, sl].astype(F32)
                fin[t, 4 * sub + sl] = part.astype(BF16).reshape(2, 32, HD)
                return carry

            lax.fori_loop(0, 4, one, 0)

    def fa_copy(t, k, jj):
        target = mod(x + k, XN)
        return pltpu.make_async_remote_copy(
            src_ref=fin.at[t, pl.ds(2 * target, 2), jj], dst_ref=dkvin.at[t, h], send_sem=fa_s.at[t, 2 * k + jj],
            recv_sem=fa_r.at[t, h], device_id=dev(z, target, 2 * x + jj), device_id_type=MESH,
        )

    def fa_start(t):
        for k in range(XN):
            for jj in range(2):
                if k:
                    fa_copy(t, k, jj).start()
                    continue
                own = h == 2 * x + jj

                @pl.when(jnp.logical_not(own))
                def _():
                    fa_copy(t, k, jj).start()

                @pl.when(own)
                def _():
                    pltpu.make_async_copy(fin.at[t, pl.ds(2 * x, 2), jj], dkvin.at[t, h], fa_r.at[t, h]).start()

    def fa_end(t):
        for hh in range(HN):
            arrived(dkvin.at[t, hh], fa_r.at[t, hh])

    def key_grads(c):
        def block(rb, carry):
            da_t = dat[c, :, lanes(rb)]
            d_row = dlt[c, pl.ds(rb, 1), :]
            for ch in range(4):
                rows = slice(ch * 256, (ch + 1) * 256)
                dp = nn_dot(vc[c, rows, :], da_t)
                ds = pmat[c, rows, lanes(rb)].astype(F32) * (dp - d_row)
                dsbuf[rows, lanes(rb)] = ds.astype(BF16)
            cols = pl.ds(pl.multiple_of(lax.rem(rb, 3) * RB, RB), RB)
            part = nn_dot(kt[c], dsbuf[:, lanes(rb)]) * INV_ROOT
            xo[1, c, rb // 3, :, cols] = part.astype(BF16)
            return carry

        lax.fori_loop(0, 6, block, 0)
        for ch in range(2):
            part = nn_dot(dsbuf[ch * 512 : (ch + 1) * 512, :], qall[c].reshape(ROWS, HD)) * INV_ROOT
            gk[c, ch * 8 : (ch + 1) * 8] = part.astype(BF16).reshape(8, PART, HD)

    rs_step(1, 0)
    rs_step(1, 1)
    key_grads(x_opp)
    xr_opp(1)
    rs_step(1, 2)
    rs_step(1, 3)
    key_grads(c_right)
    xr_near(1, 0)
    rs_step(1, 4)
    rs_step(1, 5)
    key_grads(c_left)
    xr_near(1, 1)
    rs_step(1, 6)
    xr_add(1)
    key_grads(x)
    rs_step(0, 0)
    rs_step(0, 1)
    rs_end(1)
    fa_start(1)
    rs_step(0, 2)
    rs_step(0, 3)

    xr_end(0)
    for half in range(2):
        rows = xr_rows(0, half)
        for gg in range(4):
            g = half * 4 + gg
            gated_ref[:, g * HD : (g + 1) * HD] = (rows[gg * TOK : (gg + 1) * TOK, :] * gate_ref[g]).astype(BF16)
    rs_step(0, 4)
    rs_step(0, 5)
    xr_end(1)
    for half in range(2):
        rows = xr_rows(1, half)
        for gg in range(4):
            g = half * 4 + gg
            dq_ref[:, g * HD : (g + 1) * HD] = rows[gg * TOK : (gg + 1) * TOK, :].astype(BF16)
    rs_step(0, 6)
    rs_end(0)
    fa_start(0)
    fa_end(1)
    dkv_ref[1] = dkvin[1]
    fa_end(0)
    dkv_ref[0] = dkvin[0]

    for copy in pending:
        copy.wait_send()
    for t in range(2):
        for k in range(1, HN):
            a2a_copy(t, k).wait_send()

        @pl.when(jnp.logical_not(self_in))
        def _():
            a2a_copy(t, 0).wait_send()

        for k in range(XN):
            for jj in range(2):
                if k:
                    fa_copy(t, k, jj).wait_send()
                    continue

                @pl.when(h != 2 * x + jj)
                def _():
                    fa_copy(t, k, jj).wait_send()


def on_device(queries, image_kv, gate_logit, d_gated, media_list, media_count, image_slot):
    ids = jnp.arange(SLOTS, dtype=jnp.int32)
    slots = jnp.sum(jnp.where(media_list[:, :, None] == ids, image_slot, 0), axis=-1)
    entry = jnp.arange(MEDIA, dtype=jnp.int32)
    live = entry[None, :] < media_count[:, None]
    here = (slots[:, :, None] == ids) & live[:, :, None]
    inv = jnp.sum(jnp.where(here, entry[None, :, None] + 1, 0), axis=1) - 1
    kv = image_kv.reshape(2, 32, 2, HN, HD).transpose(2, 3, 0, 1, 4)
    smem = pl.BlockSpec(memory_space=pltpu.SMEM)
    vmem = pl.BlockSpec(memory_space=pltpu.VMEM)
    dma = pltpu.SemaphoreType.DMA
    gated, d_queries, d_kv = pl.pallas_call(
        kernel,
        out_shape=(
            jax.ShapeDtypeStruct((TOK, HN * HD), BF16),
            jax.ShapeDtypeStruct((TOK, HN * HD), BF16),
            jax.ShapeDtypeStruct((2, HN, 2, 32, HD), BF16),
        ),
        in_specs=[smem] * 4 + [vmem] * 3,
        out_specs=(vmem,) * 3,
        scratch_shapes=[
            pltpu.VMEM((SLOTS, 2, 32, HD), BF16),
            pltpu.VMEM((SLOTS, 2, 32, HD), BF16),
            pltpu.VMEM((XN, 2, HALF, HD), BF16),
            pltpu.VMEM((XN, 2, HALF, HD), BF16),
            pltpu.VMEM((XN, HD, ROWS), BF16),
            pltpu.VMEM((XN, ROWS, HD), BF16),
            pltpu.VMEM((XN, KEYS, ROWS), BF16),
            pltpu.VMEM((XN, KEYS, HD), BF16),
            pltpu.VMEM((XN, HD, KEYS), BF16),
            pltpu.VMEM((XN, KEYS, HD), BF16),
            pltpu.VMEM((XN, HD, KEYS), BF16),
            pltpu.VMEM((KEYS, RB), F32),
            pltpu.VMEM((KEYS, ROWS), BF16),
            pltpu.VMEM((XN, HD, ROWS), F32),
            pltpu.VMEM((XN, 3, 8, RB), F32),
            pltpu.VMEM((XN - 1, XN, 3, 8, RB), F32),
            pltpu.VMEM((XN, 8, RB), F32),
            pltpu.VMEM((XN, 8, RB), F32),
            pltpu.VMEM((2, XN, 2, HD, HALF), BF16),
            pltpu.VMEM((2, 2, 3, HD, HALF), BF16),
            pltpu.VMEM((XN, MEDIA, PART, HD), BF16),
            pltpu.VMEM((XN, MEDIA, PART, HD), BF16),
            pltpu.VMEM((2, 2, 7, 4, PART, HD), BF16),
            pltpu.VMEM((2, 2, 7, 4, PART, HD), BF16),
            pltpu.VMEM((2, 8, 2, 32, HD), BF16),
            pltpu.VMEM((2, HN, 2, 32, HD), BF16),
            dma((2, 8)), dma((2, 8)),
            dma((2, 2, 7)), dma((2, 2, 7)),
            dma((2, 2, 3)), dma((2, 2, 3)),
            dma((4, 3)), dma((4, 3)),
            dma((2, 2, 3)), dma((2, 2, 3)),
            dma((2, 2, 7)), dma((2, 2, 7)),
            dma((2, 8)), dma((2, 8)),
        ],
        compiler_params=pltpu.CompilerParams(
            collective_id=0, has_side_effects=True, vmem_limit_bytes=60 * 1024 * 1024
        ),
        name="attend",
    )(slots, media_count, inv, jnp.tanh(gate_logit), queries, d_gated, kv)
    d_image_kv = d_kv.transpose(2, 3, 0, 1, 4).reshape(2, 32, 2, HN * HD)
    return gated, d_queries, d_image_kv


def solution(mesh):
    return jax.shard_map(
        on_device,
        mesh=mesh,
        in_specs=(
            P("seq", "head"),
            P("seq", "head", None, None),
            P("head"),
            P("seq", "head"),
            P(),
            P(),
            P(),
        ),
        out_specs=(P("seq", "head"), P("seq", "head"), P("seq", "head", None, None)),
        check_vma=False,
    )
```

time: 555 us -> 127 us (0.23)
  waiting for transfers between devices: 333 us -> 0 us
  Pallas kernels: 0 us -> 115 us
  matrix products: 101 us -> 0 us
  loops' own time: 32.9 us -> 0 us
  local copies, waits for them, and re-layouts: 29 us -> 7.93 us
  other arithmetic: 20.6 us -> 2.27 us
  between operations: 14.3 us -> 0.69 us
  blocking collectives: 12.3 us -> 0 us
  starting transfers between devices: 8.99 us -> 0 us
    reduce_scatter x1 -> x0, waiting for transfers between devices: 232 us -> none  [on_device(): lax.psum_scatter(full_grad.astype(jnp.bfloat16), 'seq', scatter_dimension...]
    pallas_call x0 -> x1, Pallas kernels: none -> 115 us  [on_device(): pl.pallas_call(kernel, out_shape=(jax.ShapeDtypeStruct((TOK, HN * HD), BF...]
    dot_general x107 -> x0, matrix products: 101 us -> none  [the longest x15 28 us: value_step(): jnp.einsum('tgv,vd->tgd', probs_low, value_rows, preferred_element_type=j...]
    all_gather x1 -> x0, waiting for transfers between devices: 96.3 us -> none  [on_device(): block_rows = lax.all_gather(by_head, 'seq', axis=0, tiled=True)]
    another operation x3 -> x0, loops' own time: 32.9 us -> none  [the longest x1 11.1 us: on_device(): lax.fori_loop(0, live_count, top_step, (top_init, total_init))]
    all_to_all x1 -> x0, blocking collectives: 12.3 us -> none  [on_device(): lax.all_to_all(image_kv, 'head', split_axis=3, concat_axis=1, tiled=True)]
    convert_element_type x1 -> x0, local copies, waits for them, and re-layouts: 12 us -> none  [on_device(): full_grad.astype(jnp.bfloat16)]
    dynamic_update_slice x15 -> x0, other arithmetic: 10 us -> none  [grad_step(): lax.dynamic_update_index_in_dim(grad_stack, both_grads, slot_index, 0)]
  transfers between devices with their start and end apart: 3 -> 0, of which waited for: 3 -> 0; matrix products, arithmetic and copies ran while one was open for 1% -> 0% of each run, Pallas kernels for 0% -> 0%
where the time goes in v1:
time: 127 us; the launch traced here: 126 us
  Pallas kernels  115 us (91%)
  local copies, waits for them, and re-layouts  7.93 us (6%)
  other arithmetic  2.27 us (2%)
    pallas_call x1, Pallas kernels, on_device(): pl.pallas_call(kernel, out_shape=(jax.ShapeDtypeStruct((TOK, HN * HD), BF...  115 us
    unnamed x15, local copies, waits for them, and re-layouts  4.86 us

profile of v1, /device:TPU:1, one launch (start us, length us, event | category | flops | bytes accessed | tf_op | source)
XLA Modules:
  0.0 126.2 jit_solution(15687007244309173854)
XLA Ops:
  0.6 0.0 copy-start.3
  0.6 1.2 tanh.3.gate_ref
  1.8 0.7 iota_compare_fusion.2
  2.5 0.0 copy-done.3
  2.6 0.0 copy-start.4
  2.6 0.1 copy.16
  2.6 0.6 copy-done.4
  3.2 0.7 select_reduce_fusion.1.slots_ref
  3.9 0.0 copy-start.2
  3.9 0.2 select_reduce_fusion
  4.2 0.4 copy-done.2
  4.5 0.6 broadcast_add_fusion.inv_ref
  5.1 1.1 reshape.42
  6.3 0.8 copy.26
  7.0 115.3 %attend.1 = (bf16[192,1024]{1,0:T(8,128)(2,1)}, bf16[192,1024]{1,0:T(8,128)(2,1)}, bf16[2,8,2,32,128]{4,3,2,1,0:T(8,128)(2,1)}) custom-call(s32[32,16]{1,0:T(8,128)} %copy-done.2, s32[32]{0:T(128)} %counts_ref.1, s32[32,64]{1,0:T(8,128)} %broadcast_add_fusion.inv_ref, f32[8]{0:T(128)} %tanh.3.gate_ref, bf16[192,1024]{1,0:T(8,128)(2,1)} %q_ref.1, ...), custom_call_target="tpu_custom_call" | custom-call | tf_op jit(solution)/shard_map/attend/pallas_call | solution.py:530
  122.3 0.0 copy-start.1
  122.3 1.2 copy.23
  123.5 0.8 reshape.43
  124.3 0.0 copy-done.1
  124.3 0.0 copy-start
  124.3 0.7 copy.29
  125.0 0.4 copy-done
  125.4 0.7 copy.30
  (1 shorter events, 0.0 us)
Async XLA Ops:
  0.6 1.9 %copy-start.3 = (s32[32,16]{0,1:T(8,128)S(1)}, s32[32,16]{0,1:T(8,128)}, u32[]{:S(2)}) copy-start(s32[32,16]{0,1:T(8,128)} %param.11) | copy-start | bytes 6148
  2.6 0.7 copy-start.4
  3.9 0.6 copy-start.2
  122.3 2.0 %copy-start.1 = (bf16[192,1024]{1,0:T(8,128)(2,1)S(1)}, bf16[192,1024]{1,0:T(8,128)(2,1)}, u32[]{:S(2)}) copy-start(bf16[192,1024]{1,0:T(8,128)(2,1)} %get-tuple-element.18) | copy-start | bytes 1179652
  124.3 1.1 copy-start

commit v2 on v1

--- a/solution.py
+++ b/solution.py
@@ -40,10 +40,10 @@
 
 
 def kernel(
-    slots_ref, counts_ref, inv_ref, gate_ref, q_ref, dg_ref, kv_ref,
+    media_ref, counts_ref, place_ref, gate_ref, q_ref, dg_ref, kv_ref,
     gated_ref, dq_ref, dkv_ref,
     kall, vall, qall, daall, dat, dap, pmat, kc, kt, vc, vt, sbuf, dsbuf, ot,
-    stat, statin, fac, dlt, xo, xin, gk, gv, rout, rin, fin, dkvin,
+    stat, statin, fac, dlt, xo, xin, gk, gv, rout, rin, fin, dkvin, inv_v, inv_ref, inv_sem,
     a2a_s, a2a_r, ag_s, ag_r, xg_s, xg_r, st_s, st_r, xr_s, xr_r, rs_s, rs_r, fa_s, fa_r,
 ):
     seq = lax.axis_index("seq")
@@ -73,7 +73,11 @@
     z_to = (mod(z + 1, ZN), mod(z - 1, ZN))
     x_to = (mod(x + 1, XN), mod(x - 1, XN))
     x_opp = mod(x + 2, XN)
-    self_in = x == hq
+    x_part = lax.rem(x + hq + 2 * hp, XN)
+    self_in = x_part == x
+
+    def holder(k, jj):
+        return 2 * ((2 * XN - k - 2 * jj) % XN) + jj
 
     barrier = pltpu.get_barrier_semaphore()
 
@@ -81,29 +85,35 @@
         pl.semaphore_signal(barrier, inc=1, device_id=device, device_id_type=MESH)
 
     for k in range(1, HN):
-        greet(dev(z, hq, mod(h + k, HN)))
+        greet(dev(z, x_part, mod(h + k, HN)))
     for k in range(1, XN):
-        greet(dev(z, mod(x + k, XN), 2 * x + hp))
-        greet(dev(z, mod(x + k, XN), 2 * x + 1 - hp))
         greet(dev(z, mod(x + k, XN), h))
-    greet(dev(z, x, 2 * x + 1 - hp))
+        for jj in range(2):
+            greet(dev(z, mod(x + k, XN), holder(k, jj)))
+    for jj in range(2):
+
+        @pl.when(h != holder(0, jj))
+        def _():
+            greet(dev(z, x, holder(0, jj)))
 
     @pl.when(jnp.logical_not(self_in))
     def _():
-        greet(dev(z, hq, h))
-        greet(dev(z, x, 2 * x + hp))
+        greet(dev(z, x_part, h))
 
     for d in range(2):
         greet(dev(z_to[d], x, h))
     pl.semaphore_wait(barrier, jnp.where(self_in, 19, 21))
+
+    def kv_lanes(t, head):
+        return kv_ref.at[:, :, pl.ds(pl.multiple_of((t * HN + head) * HD, HD), HD)]
 
     def a2a_copy(t, k):
         target = mod(h + k, HN)
         mine = kall if t == 0 else vall
         dst = mine.at[pl.ds(2 * seq, 2), hp]
         return pltpu.make_async_remote_copy(
-            src_ref=kv_ref.at[t, target], dst_ref=dst, send_sem=a2a_s.at[t, k],
-            recv_sem=a2a_r.at[t, 2 * x + hp], device_id=dev(z, hq, target), device_id_type=MESH,
+            src_ref=kv_lanes(t, target), dst_ref=dst, send_sem=a2a_s.at[t, k],
+            recv_sem=a2a_r.at[t, 2 * x + hp], device_id=dev(z, x_part, target), device_id_type=MESH,
         )
 
     for t in range(2):
@@ -117,7 +127,7 @@
         @pl.when(self_in)
         def _():
             pltpu.make_async_copy(
-                kv_ref.at[t, h], kv_all[t].at[pl.ds(2 * seq, 2), hp], a2a_r.at[t, 2 * x + hp]
+                kv_lanes(t, h), kv_all[t].at[pl.ds(2 * seq, 2), hp], a2a_r.at[t, 2 * x + hp]
             ).start()
 
     def a2a_wait(t):
@@ -162,11 +172,13 @@
             zz = mod(z - k, ZN) if d == 0 else mod(z + k, ZN)
             arrived(ag_ref(t, zz, d, pos), ag_r.at[t, d, 2 * (k - 1) + pos])
 
+    def ag_pass(t, k, pos):
+        ag_wait(t, k - 1, pos)
+        ag_send(t, k, pos)
+
     def ag_step(t, k):
         for pos in range(1 if k == 4 else 2):
-            if k > 1:
-                ag_wait(t, k - 1, pos)
-            ag_send(t, k, pos)
+            ag_pass(t, k, pos)
 
     def ag_end(t):
         ag_wait(t, 3, 1)
@@ -176,27 +188,48 @@
         rows = q_ref[:, g * HD : (g + 1) * HD]
         qall[x, g // 4, (g % 4) * TOK : (g % 4 + 1) * TOK, :] = rows
     xg_first(0)
+
+    def gate_row(g):
+        return jnp.tanh(jnp.full((1, HD), gate_ref[g], F32))
+
     for g in range(8):
-        rows = dg_ref[:, g * HD : (g + 1) * HD].astype(F32) * gate_ref[g]
+        rows = dg_ref[:, g * HD : (g + 1) * HD].astype(F32) * gate_row(g)
         daall[x, g // 4, (g % 4) * TOK : (g % 4 + 1) * TOK, :] = rows.astype(BF16)
     stat[...] = jnp.ones_like(stat)
 
+    lane = lax.broadcasted_iota(jnp.int32, (1, HD), 1)
+    inv_v[...] = jnp.full((8, HD), -1, jnp.int32)
+    for c in range(XN):
+        found = jnp.full((1, HD), -1, jnp.int32)
+        for j in range(MEDIA):
+            slot = place_ref[media_ref[j, z * XN + c]]
+            slot = jnp.where(j < counts_ref[z * XN + c], slot, -1)
+            found = jnp.where(lane == slot, j, found)
+        inv_v[c : c + 1, :] = found
+    inv_copy = pltpu.make_async_copy(inv_v, inv_ref, inv_sem)
+    inv_copy.start()
+
     a2a_wait(0)
-    ag_step(0, 1)
+    ag_send(0, 1, 0)
+    ag_send(0, 1, 1)
+    a2a_wait(1)
+    ag_send(1, 1, 0)
     xg_forward(0)
     xg_first(1)
     ag_step(0, 2)
-    a2a_wait(1)
+    ag_send(1, 1, 1)
     ag_step(0, 3)
+    ag_pass(1, 2, 0)
     ag_step(0, 4)
-    ag_step(1, 1)
+    ag_pass(1, 2, 1)
+    inv_copy.wait()
     ag_end(0)
 
     def pick(src, dst, dst_t, c):
         segment = z * XN + c
 
         def one(j, carry):
-            slot = slots_ref[segment, j]
+            slot = place_ref[media_ref[j, segment]]
             dst[c, pl.ds(pl.multiple_of(j * PART, PART), PART), :] = src[slot].reshape(PART, HD)
             return carry
 
@@ -259,14 +292,13 @@
 
     c_right, c_left = x_to
     probs_of(x)
-    ag_step(1, 2)
+    ag_step(1, 3)
     xg_wait(0, 0, 1)
     probs_of(c_left)
     xg_forward(1)
-    ag_step(1, 3)
+    ag_step(1, 4)
     xg_wait(0, 1, 1)
     probs_of(c_right)
-    ag_step(1, 4)
     for d in range(2):
         xg_wait(0, d, 2)
     probs_of(x_opp)
@@ -360,12 +392,11 @@
         lax.fori_loop(0, XN, one, 0)
 
     over_segments(value_grads)
-    xr_add(0)
 
     def own_part(t, slot):
         out = None
         for c in range(XN):
-            entry = inv_ref[z * XN + c, slot]
+            entry = inv_ref[c, slot]
             block = grads[t][c, jnp.maximum(entry, 0)].astype(F32)
             block = jnp.where(entry >= 0, block, 0.0)
             out = block if out is None else out + block
@@ -409,7 +440,7 @@
         target = mod(x + k, XN)
         return pltpu.make_async_remote_copy(
             src_ref=fin.at[t, pl.ds(2 * target, 2), jj], dst_ref=dkvin.at[t, h], send_sem=fa_s.at[t, 2 * k + jj],
-            recv_sem=fa_r.at[t, h], device_id=dev(z, target, 2 * x + jj), device_id_type=MESH,
+            recv_sem=fa_r.at[t, h], device_id=dev(z, target, holder(k, jj)), device_id_type=MESH,
         )
 
     def fa_start(t):
@@ -418,7 +449,7 @@
                 if k:
                     fa_copy(t, k, jj).start()
                     continue
-                own = h == 2 * x + jj
+                own = h == holder(0, jj)
 
                 @pl.when(jnp.logical_not(own))
                 def _():
@@ -453,6 +484,7 @@
 
     rs_step(1, 0)
     rs_step(1, 1)
+    xr_add(0)
     key_grads(x_opp)
     xr_opp(1)
     rs_step(1, 2)
@@ -478,7 +510,7 @@
         rows = xr_rows(0, half)
         for gg in range(4):
             g = half * 4 + gg
-            gated_ref[:, g * HD : (g + 1) * HD] = (rows[gg * TOK : (gg + 1) * TOK, :] * gate_ref[g]).astype(BF16)
+            gated_ref[:, g * HD : (g + 1) * HD] = (rows[gg * TOK : (gg + 1) * TOK, :] * gate_row(g)).astype(BF16)
     rs_step(0, 4)
     rs_step(0, 5)
     xr_end(1)
@@ -490,10 +522,10 @@
     rs_step(0, 6)
     rs_end(0)
     fa_start(0)
-    fa_end(1)
-    dkv_ref[1] = dkvin[1]
-    fa_end(0)
-    dkv_ref[0] = dkvin[0]
+    for t in (1, 0):
+        fa_end(t)
+        for hh in range(HN):
+            dkv_ref[:, :, (t * HN + hh) * HD : (t * HN + hh + 1) * HD] = dkvin[t, hh]
 
     for copy in pending:
         copy.wait_send()
@@ -511,19 +543,13 @@
                     fa_copy(t, k, jj).wait_send()
                     continue
 
-                @pl.when(h != 2 * x + jj)
+                @pl.when(h != holder(0, jj))
                 def _():
                     fa_copy(t, k, jj).wait_send()
 
 
 def on_device(queries, image_kv, gate_logit, d_gated, media_list, media_count, image_slot):
-    ids = jnp.arange(SLOTS, dtype=jnp.int32)
-    slots = jnp.sum(jnp.where(media_list[:, :, None] == ids, image_slot, 0), axis=-1)
-    entry = jnp.arange(MEDIA, dtype=jnp.int32)
-    live = entry[None, :] < media_count[:, None]
-    here = (slots[:, :, None] == ids) & live[:, :, None]
-    inv = jnp.sum(jnp.where(here, entry[None, :, None] + 1, 0), axis=1) - 1
-    kv = image_kv.reshape(2, 32, 2, HN, HD).transpose(2, 3, 0, 1, 4)
+    kv = image_kv.reshape(2, 32, 2 * HN * HD)
     smem = pl.BlockSpec(memory_space=pltpu.SMEM)
     vmem = pl.BlockSpec(memory_space=pltpu.VMEM)
     dma = pltpu.SemaphoreType.DMA
@@ -532,7 +558,7 @@
         out_shape=(
             jax.ShapeDtypeStruct((TOK, HN * HD), BF16),
             jax.ShapeDtypeStruct((TOK, HN * HD), BF16),
-            jax.ShapeDtypeStruct((2, HN, 2, 32, HD), BF16),
+            jax.ShapeDtypeStruct((2, 32, 2 * HN * HD), BF16),
         ),
         in_specs=[smem] * 4 + [vmem] * 3,
         out_specs=(vmem,) * 3,
@@ -563,6 +589,9 @@
             pltpu.VMEM((2, 2, 7, 4, PART, HD), BF16),
             pltpu.VMEM((2, 8, 2, 32, HD), BF16),
             pltpu.VMEM((2, HN, 2, 32, HD), BF16),
+            pltpu.VMEM((8, HD), jnp.int32),
+            pltpu.SMEM((8, HD), jnp.int32),
+            dma,
             dma((2, 8)), dma((2, 8)),
             dma((2, 2, 7)), dma((2, 2, 7)),
             dma((2, 2, 3)), dma((2, 2, 3)),
@@ -575,8 +604,8 @@
             collective_id=0, has_side_effects=True, vmem_limit_bytes=60 * 1024 * 1024
         ),
         name="attend",
-    )(slots, media_count, inv, jnp.tanh(gate_logit), queries, d_gated, kv)
-    d_image_kv = d_kv.transpose(2, 3, 0, 1, 4).reshape(2, 32, 2, HN * HD)
+    )(media_list.T, media_count, image_slot, gate_logit, queries, d_gated, kv)
+    d_image_kv = d_kv.reshape(2, 32, 2, HN * HD)
     return gated, d_queries, d_image_kv
 
 

time: 127 us -> 117 us (0.921)
  Pallas kernels: 115 us -> 110 us
  local copies, waits for them, and re-layouts: 7.93 us -> 5.62 us
  other arithmetic: 2.27 us -> 0 us
    pallas_call x1, Pallas kernels: 115 us -> 110 us  [on_device(): pl.pallas_call(kernel, out_shape=(jax.ShapeDtypeStruct((TOK, HN * HD), BF...]
    unnamed x15 -> x6, local copies, waits for them, and re-layouts: 4.86 us -> 1.89 us
    reshape x2, local copies, waits for them, and re-layouts: 1.89 us -> 3.73 us  [the longest x1 1.9 us: on_device(): d_image_kv = d_kv.reshape(2, 32, 2, HN * HD)]
where the time goes in v2:
time: 117 us; the launch traced here: 116 us
  Pallas kernels  110 us (94%)
  local copies, waits for them, and re-layouts  5.62 us (5%)
    pallas_call x1, Pallas kernels, on_device(): pl.pallas_call(kernel, out_shape=(jax.ShapeDtypeStruct((TOK, HN * HD), BF...  110 us

profile of v2, /device:TPU:1, one launch (start us, length us, event | category | flops | bytes accessed | tf_op | source)
XLA Modules:
  0.0 116.3 jit_solution(4740688004079625894)
XLA Ops:
  0.6 1.8 %reshape.12.kv_ref = bf16[2,32,2048]{2,1,0:T(8,128)(2,1)} reshape(bf16[2,32,2,1024]{3,2,1,0:T(2,128)(2,1)} %param.8) | data formatting | bytes 524288 | tf_op jit(solution)/shard_map/reshape | solution.py:552
  2.5 110.0 %attend.1 = (bf16[192,1024]{1,0:T(8,128)(2,1)}, bf16[192,1024]{1,0:T(8,128)(2,1)}, bf16[2,32,2048]{2,1,0:T(8,128)(2,1)}) custom-call(s32[16,32]{1,0:T(8,128)} %bitcast.1, s32[32]{0:T(128)} %counts_ref.1, s32[64]{0:T(128)} %place_ref.1, f32[8]{0:T(128)} %gate_ref.1, bf16[192,1024]{1,0:T(8,128)(2,1)} %q_ref.1, bf16[192,1024]{1,0:T(8,128)(2,1)} %dg_ref.1, ...), custom_call_target="tpu_custom_call" | custom-call | tf_op jit(solution)/shard_map/attend/pallas_call | solution.py:556
  112.5 0.0 copy-start.1
  112.5 1.9 %reshape.13 = bf16[2,32,2,1024]{3,2,1,0:T(2,128)(2,1)} reshape(bf16[2,32,2048]{2,1,0:T(8,128)(2,1)} %get-tuple-element.8) | data formatting | bytes 524288 | tf_op jit(solution)/shard_map/reshape | solution.py:608
  114.4 0.0 copy-done.1
  114.4 0.0 copy-start
  114.4 0.7 copy.12
  115.2 0.4 copy-done
  115.6 0.7 copy.13
Async XLA Ops:
  112.5 1.9 %copy-start.1 = (bf16[192,1024]{1,0:T(8,128)(2,1)S(1)}, bf16[192,1024]{1,0:T(8,128)(2,1)}, u32[]{:S(2)}) copy-start(bf16[192,1024]{1,0:T(8,128)(2,1)} %get-tuple-element.12) | copy-start | bytes 1179652
  114.4 1.1 copy-start

commit v3 on v2

--- a/solution.py
+++ b/solution.py
@@ -21,6 +21,8 @@
 KEYS = 1024
 PART = 64
 SLOTS = 64
+MS = 256
+UNROLL = 6
 LOG2E = 1.4426950408889634
 INV_ROOT = HD ** (-0.5)
 F32 = jnp.float32
@@ -42,7 +44,7 @@
 def kernel(
     media_ref, counts_ref, place_ref, gate_ref, q_ref, dg_ref, kv_ref,
     gated_ref, dq_ref, dkv_ref,
-    kall, vall, qall, daall, dat, dap, pmat, kc, kt, vc, vt, sbuf, dsbuf, ot,
+    kall, vall, qall, daall, dat, dap, pmat, kc, kt, vc, vt, sbuf, ot,
     stat, statin, fac, dlt, xo, xin, gk, gv, rout, rin, fin, dkvin, inv_v, inv_ref, inv_sem,
     a2a_s, a2a_r, ag_s, ag_r, xg_s, xg_r, st_s, st_r, xr_s, xr_r, rs_s, rs_r, fa_s, fa_r,
 ):
@@ -228,12 +230,9 @@
     def pick(src, dst, dst_t, c):
         segment = z * XN + c
 
-        def one(j, carry):
+        for j in range(MEDIA):
             slot = place_ref[media_ref[j, segment]]
-            dst[c, pl.ds(pl.multiple_of(j * PART, PART), PART), :] = src[slot].reshape(PART, HD)
-            return carry
-
-        lax.fori_loop(0, MEDIA, one, 0)
+            dst[c, j * PART : (j + 1) * PART, :] = src[slot].reshape(PART, HD)
         for ch in range(KEYS // 256):
             block = dst[c, ch * 256 : (ch + 1) * 256, :]
             dst_t[c, :, ch * 256 : (ch + 1) * 256] = block.T
@@ -245,43 +244,49 @@
         pick(kall, kc, kt, c)
         live = (counts_ref[z * XN + c] - LOWEST) * PART
 
-        def block(rb, carry):
-            half = rb // 3
-            q_rows = qall[c, half, pl.ds(pl.multiple_of(lax.rem(rb, 3) * RB, RB), RB), :]
-            top = None
-            for ch in range(4):
-                s = nt_dot(kc[c, ch * 256 : (ch + 1) * 256, :], q_rows)
-                if ch == 3:
-                    row_ids = lax.broadcasted_iota(jnp.int32, (256, RB), 0)
-                    s = jnp.where(row_ids < live, s, -1e30)
-                sbuf[ch * 256 : (ch + 1) * 256, :] = s
-                here = jnp.max(s, axis=0, keepdims=True)
-                top = here if top is None else jnp.maximum(top, here)
-            total = jnp.zeros((1, RB), F32)
-            for ch in range(4):
-                p = jnp.exp2((sbuf[ch * 256 : (ch + 1) * 256, :] - top) * (LOG2E * INV_ROOT))
-                total = total + jnp.sum(p, axis=0, keepdims=True)
-                pmat[c, ch * 256 : (ch + 1) * 256, lanes(rb)] = p.astype(BF16)
-            stat[c, 0, pl.ds(rb, 1), :] = top
-            stat[c, 1, pl.ds(rb, 1), :] = total
+        def block(i, carry):
+            for r in range(UNROLL):
+                rb = i * UNROLL + r
+                q_rows = qall[c, rb // 3, pl.ds(pl.multiple_of(lax.rem(rb, 3) * RB, RB), RB), :]
+                top = None
+                for m in range(KEYS // MS):
+                    rows = slice(m * MS, (m + 1) * MS)
+                    s = nt_dot(kc[c, rows, :], q_rows)
+                    if m == KEYS // MS - 1:
+                        first = LOWEST * PART - m * MS
+                        row_ids = lax.broadcasted_iota(jnp.int32, (KEYS - LOWEST * PART, RB), 0)
+                        last = jnp.where(row_ids < live, s[first:], -1e30)
+                        s = jnp.concatenate([s[:first], last], axis=0) if first else last
+                    sbuf[r, rows, :] = s
+                    here = jnp.max(s, axis=0, keepdims=True)
+                    top = here if top is None else jnp.maximum(top, here)
+                total = jnp.zeros((1, RB), F32)
+                for ch in range(4):
+                    rows = slice(ch * 256, (ch + 1) * 256)
+                    p = jnp.exp2((sbuf[r, rows, :] - top) * (LOG2E * INV_ROOT))
+                    total = total + jnp.sum(p, axis=0, keepdims=True)
+                    pmat[c, rows, lanes(rb)] = p.astype(BF16)
+                stat[c, 0, pl.ds(rb, 1), :] = top
+                stat[c, 1, pl.ds(rb, 1), :] = total
             return carry
 
-        lax.fori_loop(0, 6, block, 0)
+        lax.fori_loop(0, 6 // UNROLL, block, 0)
 
     def outs_of(c):
         pick(vall, vc, vt, c)
 
-        def block(rb, carry):
-            half = rb // 3
-            rows = daall[c, half, pl.ds(pl.multiple_of(lax.rem(rb, 3) * RB, RB), RB), :]
-            da_t = rows.T
-            dat[c, :, lanes(rb)] = da_t
-            o = nn_dot(vt[c], pmat[c, :, lanes(rb)])
-            ot[c, :, lanes(rb)] = o
-            stat[c, 2, pl.ds(rb, 1), :] = jnp.sum(da_t.astype(F32) * o, axis=0, keepdims=True)
+        def block(i, carry):
+            for r in range(UNROLL):
+                rb = i * UNROLL + r
+                rows = daall[c, rb // 3, pl.ds(pl.multiple_of(lax.rem(rb, 3) * RB, RB), RB), :]
+                da_t = rows.T
+                dat[c, :, lanes(rb)] = da_t
+                o = nn_dot(vt[c], pmat[c, :, lanes(rb)])
+                ot[c, :, lanes(rb)] = o
+                stat[c, 2, pl.ds(rb, 1), :] = jnp.sum(da_t.astype(F32) * o, axis=0, keepdims=True)
             return carry
 
-        lax.fori_loop(0, 6, block, 0)
+        lax.fori_loop(0, 6 // UNROLL, block, 0)
 
     def stat_send(c, i):
         for k in range(1, XN):
@@ -342,7 +347,7 @@
             dap[c, pl.ds(pl.multiple_of(rb * RB, RB), RB), :] = scaled.T
             return carry
 
-        lax.fori_loop(0, 6, block, 0)
+        lax.fori_loop(0, 6, block, 0, unroll=True)
 
     def xr_opp(t):
         for d in range(2):
@@ -380,9 +385,9 @@
     combine(x)
 
     def value_grads(c):
-        for ch in range(2):
-            part = nn_dot(pmat[c, ch * 512 : (ch + 1) * 512, :], dap[c])
-            gv[c, ch * 8 : (ch + 1) * 8] = part.astype(BF16).reshape(8, PART, HD)
+        for m in range(KEYS // MS):
+            part = nn_dot(pmat[c, m * MS : (m + 1) * MS, :], dap[c])
+            gv[c, m * MS // PART : (m + 1) * MS // PART] = part.astype(BF16).reshape(MS // PART, PART, HD)
 
     def over_segments(f):
         def one(c, carry):
@@ -464,64 +469,77 @@
             arrived(dkvin.at[t, hh], fa_r.at[t, hh])
 
     def key_grads(c):
-        def block(rb, carry):
-            da_t = dat[c, :, lanes(rb)]
-            d_row = dlt[c, pl.ds(rb, 1), :]
-            for ch in range(4):
-                rows = slice(ch * 256, (ch + 1) * 256)
-                dp = nn_dot(vc[c, rows, :], da_t)
-                ds = pmat[c, rows, lanes(rb)].astype(F32) * (dp - d_row)
-                dsbuf[rows, lanes(rb)] = ds.astype(BF16)
-            cols = pl.ds(pl.multiple_of(lax.rem(rb, 3) * RB, RB), RB)
-            part = nn_dot(kt[c], dsbuf[:, lanes(rb)]) * INV_ROOT
-            xo[1, c, rb // 3, :, cols] = part.astype(BF16)
+        def block(i, carry):
+            for r in range(UNROLL):
+                rb = i * UNROLL + r
+                da_t = dat[c, :, lanes(rb)]
+                d_row = dlt[c, pl.ds(rb, 1), :]
+                for m in range(KEYS // MS):
+                    rows = slice(m * MS, (m + 1) * MS)
+                    dp = nn_dot(vc[c, rows, :], da_t) - d_row
+                    ds = pmat[c, rows, lanes(rb)].astype(F32) * dp
+                    pmat[c, rows, lanes(rb)] = ds.astype(BF16)
             return carry
 
-        lax.fori_loop(0, 6, block, 0)
-        for ch in range(2):
-            part = nn_dot(dsbuf[ch * 512 : (ch + 1) * 512, :], qall[c].reshape(ROWS, HD)) * INV_ROOT
-            gk[c, ch * 8 : (ch + 1) * 8] = part.astype(BF16).reshape(8, PART, HD)
+        lax.fori_loop(0, 6 // UNROLL, block, 0)
+        for m in range(KEYS // MS):
+            part = nn_dot(pmat[c, m * MS : (m + 1) * MS, :], qall[c].reshape(ROWS, HD)) * INV_ROOT
+            gk[c, m * MS // PART : (m + 1) * MS // PART] = part.astype(BF16).reshape(MS // PART, PART, HD)
+
+    def query_grads(c):
+        def block(i, carry):
+            for r in range(UNROLL):
+                rb = i * UNROLL + r
+                part = nn_dot(kt[c], pmat[c, :, lanes(rb)]) * INV_ROOT
+                cols = pl.ds(pl.multiple_of(lax.rem(rb, 3) * RB, RB), RB)
+                xo[1, c, rb // 3, :, cols] = part.astype(BF16)
+            return carry
+
+        lax.fori_loop(0, 6 // UNROLL, block, 0)
 
     rs_step(1, 0)
     rs_step(1, 1)
     xr_add(0)
     key_grads(x_opp)
-    xr_opp(1)
     rs_step(1, 2)
     rs_step(1, 3)
     key_grads(c_right)
-    xr_near(1, 0)
     rs_step(1, 4)
+    key_grads(c_left)
     rs_step(1, 5)
-    key_grads(c_left)
-    xr_near(1, 1)
-    rs_step(1, 6)
-    xr_add(1)
     key_grads(x)
     rs_step(0, 0)
     rs_step(0, 1)
+    rs_step(1, 6)
+    query_grads(x_opp)
+    xr_opp(1)
+    query_grads(c_right)
+    xr_near(1, 0)
+    query_grads(c_left)
+    xr_near(1, 1)
+    rs_step(0, 2)
+    rs_step(0, 3)
+    query_grads(x)
     rs_end(1)
     fa_start(1)
-    rs_step(0, 2)
-    rs_step(0, 3)
-
+    rs_step(0, 4)
+    xr_add(1)
+    rs_step(0, 5)
     xr_end(0)
     for half in range(2):
         rows = xr_rows(0, half)
         for gg in range(4):
             g = half * 4 + gg
             gated_ref[:, g * HD : (g + 1) * HD] = (rows[gg * TOK : (gg + 1) * TOK, :] * gate_row(g)).astype(BF16)
-    rs_step(0, 4)
-    rs_step(0, 5)
+    rs_step(0, 6)
+    rs_end(0)
+    fa_start(0)
     xr_end(1)
     for half in range(2):
         rows = xr_rows(1, half)
         for gg in range(4):
             g = half * 4 + gg
             dq_ref[:, g * HD : (g + 1) * HD] = rows[gg * TOK : (gg + 1) * TOK, :].astype(BF16)
-    rs_step(0, 6)
-    rs_end(0)
-    fa_start(0)
     for t in (1, 0):
         fa_end(t)
         for hh in range(HN):
@@ -574,8 +592,7 @@
             pltpu.VMEM((XN, HD, KEYS), BF16),
             pltpu.VMEM((XN, KEYS, HD), BF16),
             pltpu.VMEM((XN, HD, KEYS), BF16),
-            pltpu.VMEM((KEYS, RB), F32),
-            pltpu.VMEM((KEYS, ROWS), BF16),
+            pltpu.VMEM((UNROLL, KEYS, RB), F32),
             pltpu.VMEM((XN, HD, ROWS), F32),
             pltpu.VMEM((XN, 3, 8, RB), F32),
             pltpu.VMEM((XN - 1, XN, 3, 8, RB), F32),

time: 117 us -> 100 us (0.85)
  Pallas kernels: 110 us -> 93.8 us
    pallas_call x1, Pallas kernels: 110 us -> 93.8 us  [on_device(): pl.pallas_call(kernel, out_shape=(jax.ShapeDtypeStruct((TOK, HN * HD), BF...]
where the time goes in v3:
time: 100 us
  Pallas kernels  93.8 us (94%)
  local copies, waits for them, and re-layouts  5.62 us (6%)
    pallas_call x1, Pallas kernels, on_device(): pl.pallas_call(kernel, out_shape=(jax.ShapeDtypeStruct((TOK, HN * HD), BF...  93.8 us

profile of v3, /device:TPU:1, one launch (start us, length us, event | category | flops | bytes accessed | tf_op | source)
XLA Modules:
  0.0 100.0 jit_solution(8279187233858424665)
XLA Ops:
  0.6 1.8 %reshape.12.kv_ref = bf16[2,32,2048]{2,1,0:T(8,128)(2,1)} reshape(bf16[2,32,2,1024]{3,2,1,0:T(2,128)(2,1)} %param.8) | data formatting | bytes 524288 | tf_op jit(solution)/shard_map/reshape | solution.py:570
  2.5 93.8 %attend.1 = (bf16[192,1024]{1,0:T(8,128)(2,1)}, bf16[192,1024]{1,0:T(8,128)(2,1)}, bf16[2,32,2048]{2,1,0:T(8,128)(2,1)}) custom-call(s32[16,32]{1,0:T(8,128)} %bitcast.1, s32[32]{0:T(128)} %counts_ref.1, s32[64]{0:T(128)} %place_ref.1, f32[8]{0:T(128)} %gate_ref.1, bf16[192,1024]{1,0:T(8,128)(2,1)} %q_ref.1, bf16[192,1024]{1,0:T(8,128)(2,1)} %dg_ref.1, ...), custom_call_target="tpu_custom_call" | custom-call | tf_op jit(solution)/shard_map/attend/pallas_call | solution.py:574
  96.2 0.0 copy-start.1
  96.2 1.9 %reshape.13 = bf16[2,32,2,1024]{3,2,1,0:T(2,128)(2,1)} reshape(bf16[2,32,2048]{2,1,0:T(8,128)(2,1)} %get-tuple-element.8) | data formatting | bytes 524288 | tf_op jit(solution)/shard_map/reshape | solution.py:625
  98.1 0.0 copy-done.1
  98.1 0.0 copy-start
  98.1 0.7 copy.12
  98.9 0.4 copy-done
  99.3 0.7 copy.13
Async XLA Ops:
  96.2 1.9 %copy-start.1 = (bf16[192,1024]{1,0:T(8,128)(2,1)S(1)}, bf16[192,1024]{1,0:T(8,128)(2,1)}, u32[]{:S(2)}) copy-start(bf16[192,1024]{1,0:T(8,128)(2,1)} %get-tuple-element.12) | copy-start | bytes 1179652
  98.1 1.1 %copy-start = (bf16[192,1024]{1,0:T(8,128)(2,1)S(1)}, bf16[192,1024]{1,0:T(8,128)(2,1)}, u32[]{:S(2)}) copy-start(bf16[192,1024]{1,0:T(8,128)(2,1)} %get-tuple-element.13) | copy-start | bytes 1179652

commit v4 on v3

--- a/solution.py
+++ b/solution.py
@@ -132,8 +132,8 @@
                 kv_lanes(t, h), kv_all[t].at[pl.ds(2 * seq, 2), hp], a2a_r.at[t, 2 * x + hp]
             ).start()
 
-    def a2a_wait(t):
-        for xx in range(XN):
+    def a2a_wait(t, sub):
+        for xx in (2 * sub, 2 * sub + 1):
             for jj in range(2):
                 arrived(kv_all[t].at[pl.ds(2 * (z * XN + xx), 2), jj], a2a_r.at[t, 2 * xx + jj])
 
@@ -162,8 +162,8 @@
         sub = d if pos == 0 else 1 - d
         return kv_all[t].at[pl.ds(zz * 8 + 4 * sub, 4)]
 
-    def ag_send(t, k, pos):
-        for d in range(2):
+    def ag_send(t, k, pos, ways=(0, 1)):
+        for d in ways:
             zz = mod(z - (k - 1), ZN) if d == 0 else mod(z + (k - 1), ZN)
             ref = ag_ref(t, zz, d, pos)
             i = 2 * (k - 1) + pos
@@ -211,11 +211,13 @@
     inv_copy = pltpu.make_async_copy(inv_v, inv_ref, inv_sem)
     inv_copy.start()
 
-    a2a_wait(0)
-    ag_send(0, 1, 0)
-    ag_send(0, 1, 1)
-    a2a_wait(1)
-    ag_send(1, 1, 0)
+    for t in range(2):
+        a2a_wait(t, 0)
+        ag_send(t, 1, 0, (0,))
+        a2a_wait(t, 1)
+        ag_send(t, 1, 0, (1,))
+        if t == 0:
+            ag_send(0, 1, 1)
     xg_forward(0)
     xg_first(1)
     ag_step(0, 2)
@@ -272,15 +274,19 @@
 
         lax.fori_loop(0, 6 // UNROLL, block, 0)
 
+    def turn(c):
+        for half in range(2):
+            for r in range(3):
+                rb = half * 3 + r
+                dat[c, :, rb * RB : (rb + 1) * RB] = daall[c, half, r * RB : (r + 1) * RB, :].T
+
     def outs_of(c):
         pick(vall, vc, vt, c)
 
         def block(i, carry):
             for r in range(UNROLL):
                 rb = i * UNROLL + r
-                rows = daall[c, rb // 3, pl.ds(pl.multiple_of(lax.rem(rb, 3) * RB, RB), RB), :]
-                da_t = rows.T
-                dat[c, :, lanes(rb)] = da_t
+                da_t = dat[c, :, lanes(rb)]
                 o = nn_dot(vt[c], pmat[c, :, lanes(rb)])
                 ot[c, :, lanes(rb)] = o
                 stat[c, 2, pl.ds(rb, 1), :] = jnp.sum(da_t.astype(F32) * o, axis=0, keepdims=True)
@@ -296,36 +302,37 @@
             )
 
     c_right, c_left = x_to
+    xg_forward(1)
+    turn(x)
     probs_of(x)
     ag_step(1, 3)
     xg_wait(0, 0, 1)
     probs_of(c_left)
-    xg_forward(1)
     ag_step(1, 4)
     xg_wait(0, 1, 1)
     probs_of(c_right)
     for d in range(2):
         xg_wait(0, d, 2)
     probs_of(x_opp)
-    ag_end(1)
-
-    outs_of(x)
-    stat_send(x, 0)
     xg_wait(1, 0, 1)
-    outs_of(c_left)
-    stat_send(c_left, 1)
+    turn(c_left)
     xg_wait(1, 1, 1)
-    outs_of(c_right)
-    stat_send(c_right, 2)
+    turn(c_right)
     for d in range(2):
         xg_wait(1, d, 2)
-    outs_of(x_opp)
-    stat_send(x_opp, 3)
-    for i, off in enumerate((0, -1, 1, 2)):
+    turn(x_opp)
+    ag_end(1)
+
+    for c in range(XN):
+        outs_of(c)
+        stat_send(c, c)
+
+    def stat_wait(c):
         for k in range(1, XN):
-            arrived(statin.at[k - 1, mod(x - k + off + XN, XN)], st_r.at[i, k - 1])
+            arrived(statin.at[k - 1, c], st_r.at[c, k - 1])
 
     def combine(c):
+        stat_wait(c)
         tops = [stat[c, 0]] + [statin[k, c, 0] for k in range(XN - 1)]
         totals = [stat[c, 1]] + [statin[k, c, 1] for k in range(XN - 1)]
         dots = [stat[c, 2]] + [statin[k, c, 2] for k in range(XN - 1)]
@@ -376,13 +383,11 @@
         both = xo[t, x, half].astype(F32) + xin[t, half, 2].astype(F32) + xin[t, 1 - half, 1].astype(F32)
         return both.T
 
-    combine(x_opp)
+    for c in range(XN):
+        combine(c)
     xr_opp(0)
-    combine(c_right)
     xr_near(0, 0)
-    combine(c_left)
     xr_near(0, 1)
-    combine(x)
 
     def value_grads(c):
         for m in range(KEYS // MS):
@@ -499,10 +504,12 @@
 
     rs_step(1, 0)
     rs_step(1, 1)
+    key_grads(x_opp)
     xr_add(0)
-    key_grads(x_opp)
     rs_step(1, 2)
     rs_step(1, 3)
+    query_grads(x_opp)
+    xr_opp(1)
     key_grads(c_right)
     rs_step(1, 4)
     key_grads(c_left)
@@ -511,19 +518,17 @@
     rs_step(0, 0)
     rs_step(0, 1)
     rs_step(1, 6)
-    query_grads(x_opp)
-    xr_opp(1)
     query_grads(c_right)
     xr_near(1, 0)
     query_grads(c_left)
     xr_near(1, 1)
     rs_step(0, 2)
     rs_step(0, 3)
+    xr_add(1)
     query_grads(x)
     rs_end(1)
     fa_start(1)
     rs_step(0, 4)
-    xr_add(1)
     rs_step(0, 5)
     xr_end(0)
     for half in range(2):

time: 100 us -> 100 us (level)
  no operation moved by 1% of the time
where the time goes in v4:
time: 100 us
  Pallas kernels  93.8 us (94%)
  local copies, waits for them, and re-layouts  5.62 us (6%)
    pallas_call x1, Pallas kernels, on_device(): pl.pallas_call(kernel, out_shape=(jax.ShapeDtypeStruct((TOK, HN * HD), BF...  93.8 us

profile of v4, /device:TPU:1, one launch (start us, length us, event | category | flops | bytes accessed | tf_op | source)
XLA Modules:
  0.0 100.1 jit_solution(5295447617373875088)
XLA Ops:
  0.6 1.8 %reshape.12.kv_ref = bf16[2,32,2048]{2,1,0:T(8,128)(2,1)} reshape(bf16[2,32,2,1024]{3,2,1,0:T(2,128)(2,1)} %param.8) | data formatting | bytes 524288 | tf_op jit(solution)/shard_map/reshape | solution.py:575
  2.5 93.8 %attend.1 = (bf16[192,1024]{1,0:T(8,128)(2,1)}, bf16[192,1024]{1,0:T(8,128)(2,1)}, bf16[2,32,2048]{2,1,0:T(8,128)(2,1)}) custom-call(s32[16,32]{1,0:T(8,128)} %bitcast.1, s32[32]{0:T(128)} %counts_ref.1, s32[64]{0:T(128)} %place_ref.1, f32[8]{0:T(128)} %gate_ref.1, bf16[192,1024]{1,0:T(8,128)(2,1)} %q_ref.1, bf16[192,1024]{1,0:T(8,128)(2,1)} %dg_ref.1, ...), custom_call_target="tpu_custom_call" | custom-call | tf_op jit(solution)/shard_map/attend/pallas_call | solution.py:579
  96.3 0.0 copy-start.1
  96.3 1.9 %reshape.13 = bf16[2,32,2,1024]{3,2,1,0:T(2,128)(2,1)} reshape(bf16[2,32,2048]{2,1,0:T(8,128)(2,1)} %get-tuple-element.8) | data formatting | bytes 524288 | tf_op jit(solution)/shard_map/reshape | solution.py:630
  98.2 0.0 copy-done.1
  98.2 0.0 copy-start
  98.2 0.7 copy.12
  98.9 0.4 copy-done
  99.3 0.7 copy.13
Async XLA Ops:
  96.3 1.9 %copy-start.1 = (bf16[192,1024]{1,0:T(8,128)(2,1)S(1)}, bf16[192,1024]{1,0:T(8,128)(2,1)}, u32[]{:S(2)}) copy-start(bf16[192,1024]{1,0:T(8,128)(2,1)} %get-tuple-element.12) | copy-start | bytes 1179652
  98.2 1.1 %copy-start = (bf16[192,1024]{1,0:T(8,128)(2,1)S(1)}, bf16[192,1024]{1,0:T(8,128)(2,1)}, u32[]{:S(2)}) copy-start(bf16[192,1024]{1,0:T(8,128)(2,1)} %get-tuple-element.13) | copy-start | bytes 1179652

commit v5 on v4

--- a/solution.py
+++ b/solution.py
@@ -45,7 +45,7 @@
     media_ref, counts_ref, place_ref, gate_ref, q_ref, dg_ref, kv_ref,
     gated_ref, dq_ref, dkv_ref,
     kall, vall, qall, daall, dat, dap, pmat, kc, kt, vc, vt, sbuf, ot,
-    stat, statin, fac, dlt, xo, xin, gk, gv, rout, rin, fin, dkvin, inv_v, inv_ref, inv_sem,
+    stat, statin, fac, dlt, xo, xin, gk, gv, rout, rin, sums, fin, dkvin, inv_v, inv_ref, inv_sem,
     a2a_s, a2a_r, ag_s, ag_r, xg_s, xg_r, st_s, st_r, xr_s, xr_r, rs_s, rs_r, fa_s, fa_r,
 ):
     seq = lax.axis_index("seq")
@@ -412,6 +412,15 @@
             out = block if out is None else out + block
         return out
 
+    def rs_prep(t):
+        def one(i, carry):
+            for r in range(8):
+                slot = i * 8 + r
+                sums[t, slot] = own_part(t, slot)
+            return carry
+
+        lax.fori_loop(0, SLOTS // 8, one, 0)
+
     def rs_step(t, i):
         k = (i + 3) // 2
         for d in range(2):
@@ -421,14 +430,13 @@
             if i >= 2:
                 arrived(rin.at[t, d, i - 2], rs_r.at[t, d, i - 2])
 
-            def one(sl, carry):
-                part = own_part(t, zt * 8 + 4 * sub + sl)
-                if i >= 2:
-                    part = part + rin[t, d, i - 2, sl].astype(F32)
-                rout[t, d, i, sl] = part.astype(BF16)
-                return carry
-
-            lax.fori_loop(0, 4, one, 0)
+            first = zt * 8 + 4 * sub
+            if i < 2:
+                for sl in range(4):
+                    rout[t, d, i, sl] = own_part(t, first + sl).astype(BF16)
+            else:
+                both = sums[t, pl.ds(first, 4)] + rin[t, d, i - 2].astype(F32)
+                rout[t, d, i] = both.astype(BF16)
             send(rout.at[t, d, i], rin.at[t, d, i], rs_s.at[t, d, i], rs_r.at[t, d, i], dev(z_to[d], x, h))
 
     def rs_end(t):
@@ -436,15 +444,10 @@
             for d in range(2):
                 arrived(rin.at[t, d, i], rs_r.at[t, d, i])
         for sub in range(2):
-
-            def one(sl, carry):
-                part = own_part(t, z * 8 + 4 * sub + sl)
-                for d in range(2):
-                    part = part + rin[t, d, 6 if sub == d else 5, sl].astype(F32)
-                fin[t, 4 * sub + sl] = part.astype(BF16).reshape(2, 32, HD)
-                return carry
-
-            lax.fori_loop(0, 4, one, 0)
+            part = sums[t, pl.ds(z * 8 + 4 * sub, 4)]
+            for d in range(2):
+                part = part + rin[t, d, 6 if sub == d else 5].astype(F32)
+            fin[t, 4 * sub : 4 * sub + 4] = part.astype(BF16).reshape(4, 2, 32, HD)
 
     def fa_copy(t, k, jj):
         target = mod(x + k, XN)
@@ -504,13 +507,14 @@
 
     rs_step(1, 0)
     rs_step(1, 1)
+    rs_prep(1)
     key_grads(x_opp)
+    rs_step(1, 2)
     xr_add(0)
-    rs_step(1, 2)
+    key_grads(c_right)
     rs_step(1, 3)
     query_grads(x_opp)
     xr_opp(1)
-    key_grads(c_right)
     rs_step(1, 4)
     key_grads(c_left)
     rs_step(1, 5)
@@ -518,17 +522,18 @@
     rs_step(0, 0)
     rs_step(0, 1)
     rs_step(1, 6)
+    rs_prep(0)
     query_grads(c_right)
     xr_near(1, 0)
     query_grads(c_left)
     xr_near(1, 1)
     rs_step(0, 2)
     rs_step(0, 3)
-    xr_add(1)
-    query_grads(x)
     rs_end(1)
     fa_start(1)
+    query_grads(x)
     rs_step(0, 4)
+    xr_add(1)
     rs_step(0, 5)
     xr_end(0)
     for half in range(2):
@@ -609,6 +614,7 @@
             pltpu.VMEM((XN, MEDIA, PART, HD), BF16),
             pltpu.VMEM((2, 2, 7, 4, PART, HD), BF16),
             pltpu.VMEM((2, 2, 7, 4, PART, HD), BF16),
+            pltpu.VMEM((2, SLOTS, PART, HD), F32),
             pltpu.VMEM((2, 8, 2, 32, HD), BF16),
             pltpu.VMEM((2, HN, 2, 32, HD), BF16),
             pltpu.VMEM((8, HD), jnp.int32),

time: 100 us -> 99.2 us (level)
  Pallas kernels: 93.8 us -> 92.8 us
    pallas_call x1, Pallas kernels: 93.8 us -> 92.8 us  [on_device(): pl.pallas_call(kernel, out_shape=(jax.ShapeDtypeStruct((TOK, HN * HD), BF...]
where the time goes in v5:
time: 99.2 us; the launch traced here: 99 us
  Pallas kernels  92.8 us (94%)
  local copies, waits for them, and re-layouts  5.62 us (6%)
    pallas_call x1, Pallas kernels, on_device(): pl.pallas_call(kernel, out_shape=(jax.ShapeDtypeStruct((TOK, HN * HD), BF...  92.8 us

profile of v5, /device:TPU:1, one launch (start us, length us, event | category | flops | bytes accessed | tf_op | source)
XLA Modules:
  0.0 99.0 jit_solution(8841663066539428339)
XLA Ops:
  0.6 1.8 %reshape.12.kv_ref = bf16[2,32,2048]{2,1,0:T(8,128)(2,1)} reshape(bf16[2,32,2,1024]{3,2,1,0:T(2,128)(2,1)} %param.8) | data formatting | bytes 524288 | tf_op jit(solution)/shard_map/reshape | solution.py:580
  2.5 92.8 %attend.1 = (bf16[192,1024]{1,0:T(8,128)(2,1)}, bf16[192,1024]{1,0:T(8,128)(2,1)}, bf16[2,32,2048]{2,1,0:T(8,128)(2,1)}) custom-call(s32[16,32]{1,0:T(8,128)} %bitcast.1, s32[32]{0:T(128)} %counts_ref.1, s32[64]{0:T(128)} %place_ref.1, f32[8]{0:T(128)} %gate_ref.1, bf16[192,1024]{1,0:T(8,128)(2,1)} %q_ref.1, bf16[192,1024]{1,0:T(8,128)(2,1)} %dg_ref.1, ...), custom_call_target="tpu_custom_call" | custom-call | tf_op jit(solution)/shard_map/attend/pallas_call | solution.py:584
  95.2 0.0 copy-start.1
  95.2 1.9 %reshape.13 = bf16[2,32,2,1024]{3,2,1,0:T(2,128)(2,1)} reshape(bf16[2,32,2048]{2,1,0:T(8,128)(2,1)} %get-tuple-element.8) | data formatting | bytes 524288 | tf_op jit(solution)/shard_map/reshape | solution.py:636
  97.1 0.0 copy-done.1
  97.1 0.0 copy-start
  97.1 0.7 copy.12
  97.9 0.4 copy-done
  98.3 0.7 copy.13
Async XLA Ops:
  95.2 1.9 %copy-start.1 = (bf16[192,1024]{1,0:T(8,128)(2,1)S(1)}, bf16[192,1024]{1,0:T(8,128)(2,1)}, u32[]{:S(2)}) copy-start(bf16[192,1024]{1,0:T(8,128)(2,1)} %get-tuple-element.12) | copy-start | bytes 1179652
  97.1 1.1 %copy-start = (bf16[192,1024]{1,0:T(8,128)(2,1)S(1)}, bf16[192,1024]{1,0:T(8,128)(2,1)}, u32[]{:S(2)}) copy-start(bf16[192,1024]{1,0:T(8,128)(2,1)} %get-tuple-element.13) | copy-start | bytes 1179652

commit v6 on v5

--- a/solution.py
+++ b/solution.py
@@ -45,7 +45,7 @@
     media_ref, counts_ref, place_ref, gate_ref, q_ref, dg_ref, kv_ref,
     gated_ref, dq_ref, dkv_ref,
     kall, vall, qall, daall, dat, dap, pmat, kc, kt, vc, vt, sbuf, ot,
-    stat, statin, fac, dlt, xo, xin, gk, gv, rout, rin, sums, fin, dkvin, inv_v, inv_ref, inv_sem,
+    stat, statin, fac, dlt, xo, xin, gk, gv, rout, rin, sums, fin, dkvin, kvlin, inv_v, inv_ref, inv_sem,
     a2a_s, a2a_r, ag_s, ag_r, xg_s, xg_r, st_s, st_r, xr_s, xr_r, rs_s, rs_r, fa_s, fa_r,
 ):
     seq = lax.axis_index("seq")
@@ -104,92 +104,12 @@
 
     for d in range(2):
         greet(dev(z_to[d], x, h))
-    pl.semaphore_wait(barrier, jnp.where(self_in, 19, 21))
-
-    def kv_lanes(t, head):
-        return kv_ref.at[:, :, pl.ds(pl.multiple_of((t * HN + head) * HD, HD), HD)]
-
-    def a2a_copy(t, k):
-        target = mod(h + k, HN)
-        mine = kall if t == 0 else vall
-        dst = mine.at[pl.ds(2 * seq, 2), hp]
-        return pltpu.make_async_remote_copy(
-            src_ref=kv_lanes(t, target), dst_ref=dst, send_sem=a2a_s.at[t, k],
-            recv_sem=a2a_r.at[t, 2 * x + hp], device_id=dev(z, x_part, target), device_id_type=MESH,
-        )
-
-    for t in range(2):
-        for k in range(1, HN):
-            a2a_copy(t, k).start()
-
-        @pl.when(jnp.logical_not(self_in))
-        def _():
-            a2a_copy(t, 0).start()
-
-        @pl.when(self_in)
-        def _():
-            pltpu.make_async_copy(
-                kv_lanes(t, h), kv_all[t].at[pl.ds(2 * seq, 2), hp], a2a_r.at[t, 2 * x + hp]
-            ).start()
-
-    def a2a_wait(t, sub):
-        for xx in (2 * sub, 2 * sub + 1):
-            for jj in range(2):
-                arrived(kv_all[t].at[pl.ds(2 * (z * XN + xx), 2), jj], a2a_r.at[t, 2 * xx + jj])
-
-    def xg_ref(t, c, half):
-        return xg_all[t].at[c, half]
-
-    def xg_first(t):
-        for pos in range(2):
-            for d in range(2):
-                half = d if pos == 0 else 1 - d
-                ref = xg_ref(t, x, half)
-                send(ref, ref, xg_s.at[t, d, pos], xg_r.at[t, d, pos], dev(z, x_to[d], h))
-
-    def xg_wait(t, d, pos):
-        c = x_opp if pos == 2 else x_to[1 - d]
-        half = 1 - d if pos == 1 else d
-        arrived(xg_ref(t, c, half), xg_r.at[t, d, pos])
-
-    def xg_forward(t):
-        for d in range(2):
-            xg_wait(t, d, 0)
-            ref = xg_ref(t, x_to[1 - d], d)
-            send(ref, ref, xg_s.at[t, d, 2], xg_r.at[t, d, 2], dev(z, x_to[d], h))
-
-    def ag_ref(t, zz, d, pos):
-        sub = d if pos == 0 else 1 - d
-        return kv_all[t].at[pl.ds(zz * 8 + 4 * sub, 4)]
-
-    def ag_send(t, k, pos, ways=(0, 1)):
-        for d in ways:
-            zz = mod(z - (k - 1), ZN) if d == 0 else mod(z + (k - 1), ZN)
-            ref = ag_ref(t, zz, d, pos)
-            i = 2 * (k - 1) + pos
-            send(ref, ref, ag_s.at[t, d, i], ag_r.at[t, d, i], dev(z_to[d], x, h))
-
-    def ag_wait(t, k, pos):
-        for d in range(2):
-            zz = mod(z - k, ZN) if d == 0 else mod(z + k, ZN)
-            arrived(ag_ref(t, zz, d, pos), ag_r.at[t, d, 2 * (k - 1) + pos])
-
-    def ag_pass(t, k, pos):
-        ag_wait(t, k - 1, pos)
-        ag_send(t, k, pos)
-
-    def ag_step(t, k):
-        for pos in range(1 if k == 4 else 2):
-            ag_pass(t, k, pos)
-
-    def ag_end(t):
-        ag_wait(t, 3, 1)
-        ag_wait(t, 4, 0)
-
+    for i in range(2):
+        for t in range(2):
+            kvlin[i, :, t * HN * HD : (t + 1) * HN * HD] = kv_ref[i, :, t, :]
     for g in range(8):
         rows = q_ref[:, g * HD : (g + 1) * HD]
         qall[x, g // 4, (g % 4) * TOK : (g % 4 + 1) * TOK, :] = rows
-    xg_first(0)
 
     def gate_row(g):
         return jnp.tanh(jnp.full((1, HD), gate_ref[g], F32))
@@ -209,6 +129,90 @@
             found = jnp.where(lane == slot, j, found)
         inv_v[c : c + 1, :] = found
     inv_copy = pltpu.make_async_copy(inv_v, inv_ref, inv_sem)
+
+    pl.semaphore_wait(barrier, jnp.where(self_in, 19, 21))
+
+    def kv_lanes(t, head):
+        return kvlin.at[:, :, pl.ds(pl.multiple_of((t * HN + head) * HD, HD), HD)]
+
+    def a2a_copy(t, k):
+        target = mod(h + k, HN)
+        mine = kall if t == 0 else vall
+        dst = mine.at[pl.ds(2 * seq, 2), hp]
+        return pltpu.make_async_remote_copy(
+            src_ref=kv_lanes(t, target), dst_ref=dst, send_sem=a2a_s.at[t, k],
+            recv_sem=a2a_r.at[t, 2 * x + hp], device_id=dev(z, x_part, target), device_id_type=MESH,
+        )
+
+    for t in range(2):
+        for k in range(1, HN):
+            a2a_copy(t, k).start()
+
+        @pl.when(jnp.logical_not(self_in))
+        def _():
+            a2a_copy(t, 0).start()
+
+        @pl.when(self_in)
+        def _():
+            pltpu.make_async_copy(
+                kv_lanes(t, h), kv_all[t].at[pl.ds(2 * seq, 2), hp], a2a_r.at[t, 2 * x + hp]
+            ).start()
+
+    def a2a_wait(t, sub):
+        for xx in (2 * sub, 2 * sub + 1):
+            for jj in range(2):
+                arrived(kv_all[t].at[pl.ds(2 * (z * XN + xx), 2), jj], a2a_r.at[t, 2 * xx + jj])
+
+    def xg_ref(t, c, half):
+        return xg_all[t].at[c, half]
+
+    def xg_first(t):
+        for pos in range(2):
+            for d in range(2):
+                half = d if pos == 0 else 1 - d
+                ref = xg_ref(t, x, half)
+                send(ref, ref, xg_s.at[t, d, pos], xg_r.at[t, d, pos], dev(z, x_to[d], h))
+
+    def xg_wait(t, d, pos):
+        c = x_opp if pos == 2 else x_to[1 - d]
+        half = 1 - d if pos == 1 else d
+        arrived(xg_ref(t, c, half), xg_r.at[t, d, pos])
+
+    def xg_forward(t):
+        for d in range(2):
+            xg_wait(t, d, 0)
+            ref = xg_ref(t, x_to[1 - d], d)
+            send(ref, ref, xg_s.at[t, d, 2], xg_r.at[t, d, 2], dev(z, x_to[d], h))
+
+    def ag_ref(t, zz, d, pos):
+        sub = d if pos == 0 else 1 - d
+        return kv_all[t].at[pl.ds(zz * 8 + 4 * sub, 4)]
+
+    def ag_send(t, k, pos, ways=(0, 1)):
+        for d in ways:
+            zz = mod(z - (k - 1), ZN) if d == 0 else mod(z + (k - 1), ZN)
+            ref = ag_ref(t, zz, d, pos)
+            i = 2 * (k - 1) + pos
+            send(ref, ref, ag_s.at[t, d, i], ag_r.at[t, d, i], dev(z_to[d], x, h))
+
+    def ag_wait(t, k, pos):
+        for d in range(2):
+            zz = mod(z - k, ZN) if d == 0 else mod(z + k, ZN)
+            arrived(ag_ref(t, zz, d, pos), ag_r.at[t, d, 2 * (k - 1) + pos])
+
+    def ag_pass(t, k, pos):
+        ag_wait(t, k - 1, pos)
+        ag_send(t, k, pos)
+
+    def ag_step(t, k):
+        for pos in range(1 if k == 4 else 2):
+            ag_pass(t, k, pos)
+
+    def ag_end(t):
+        ag_wait(t, 3, 1)
+        ag_wait(t, 4, 0)
+
+    xg_first(0)
     inv_copy.start()
 
     for t in range(2):
@@ -422,32 +426,33 @@
         lax.fori_loop(0, SLOTS // 8, one, 0)
 
     def rs_step(t, i):
-        k = (i + 3) // 2
-        for d in range(2):
-            away = 5 - k
-            zt = mod(z + away, ZN) if d == 0 else mod(z - away, ZN)
-            sub = d if i % 2 == 0 else 1 - d
-            if i >= 2:
-                arrived(rin.at[t, d, i - 2], rs_r.at[t, d, i - 2])
-
-            first = zt * 8 + 4 * sub
-            if i < 2:
-                for sl in range(4):
-                    rout[t, d, i, sl] = own_part(t, first + sl).astype(BF16)
-            else:
-                both = sums[t, pl.ds(first, 4)] + rin[t, d, i - 2].astype(F32)
-                rout[t, d, i] = both.astype(BF16)
-            send(rout.at[t, d, i], rin.at[t, d, i], rs_s.at[t, d, i], rs_r.at[t, d, i], dev(z_to[d], x, h))
+        away = 5 - (i + 3) // 2
+        for m in range(2):
+            for d in range(2):
+                zt = mod(z + away, ZN) if d == 0 else mod(z - away, ZN)
+                sub = d if i % 2 == 0 else 1 - d
+                first = zt * 8 + 4 * sub + 2 * m
+                j = 2 * i + m
+                if i < 2:
+                    for sl in range(2):
+                        rout[t, d, j, sl] = own_part(t, first + sl).astype(BF16)
+                else:
+                    arrived(rin.at[t, d, j - 4], rs_r.at[t, d, j - 4])
+                    both = sums[t, pl.ds(first, 2)] + rin[t, d, j - 4].astype(F32)
+                    rout[t, d, j] = both.astype(BF16)
+                send(rout.at[t, d, j], rin.at[t, d, j], rs_s.at[t, d, j], rs_r.at[t, d, j], dev(z_to[d], x, h))
 
     def rs_end(t):
-        for i in (5, 6):
+        for j in range(10, 14):
             for d in range(2):
-                arrived(rin.at[t, d, i], rs_r.at[t, d, i])
+                arrived(rin.at[t, d, j], rs_r.at[t, d, j])
         for sub in range(2):
-            part = sums[t, pl.ds(z * 8 + 4 * sub, 4)]
-            for d in range(2):
-                part = part + rin[t, d, 6 if sub == d else 5].astype(F32)
-            fin[t, 4 * sub : 4 * sub + 4] = part.astype(BF16).reshape(4, 2, 32, HD)
+            for m in range(2):
+                first = 4 * sub + 2 * m
+                part = sums[t, pl.ds(z * 8 + first, 2)]
+                for d in range(2):
+                    part = part + rin[t, d, (12 if sub == d else 10) + m].astype(F32)
+                fin[t, first : first + 2] = part.astype(BF16).reshape(2, 2, 32, HD)
 
     def fa_copy(t, k, jj):
         target = mod(x + k, XN)
@@ -509,19 +514,17 @@
     rs_step(1, 1)
     rs_prep(1)
     key_grads(x_opp)
+    key_grads(c_right)
     rs_step(1, 2)
     xr_add(0)
-    key_grads(c_right)
     rs_step(1, 3)
     query_grads(x_opp)
     xr_opp(1)
-    rs_step(1, 4)
     key_grads(c_left)
-    rs_step(1, 5)
     key_grads(x)
     rs_step(0, 0)
     rs_step(0, 1)
-    rs_step(1, 6)
+    rs_step(1, 4)
     rs_prep(0)
     query_grads(c_right)
     xr_near(1, 0)
@@ -529,12 +532,12 @@
     xr_near(1, 1)
     rs_step(0, 2)
     rs_step(0, 3)
-    rs_end(1)
-    fa_start(1)
+    rs_step(1, 5)
     query_grads(x)
     rs_step(0, 4)
+    rs_step(0, 5)
+    rs_step(1, 6)
     xr_add(1)
-    rs_step(0, 5)
     xr_end(0)
     for half in range(2):
         rows = xr_rows(0, half)
@@ -542,6 +545,8 @@
             g = half * 4 + gg
             gated_ref[:, g * HD : (g + 1) * HD] = (rows[gg * TOK : (gg + 1) * TOK, :] * gate_row(g)).astype(BF16)
     rs_step(0, 6)
+    rs_end(1)
+    fa_start(1)
     rs_end(0)
     fa_start(0)
     xr_end(1)
@@ -553,7 +558,7 @@
     for t in (1, 0):
         fa_end(t)
         for hh in range(HN):
-            dkv_ref[:, :, (t * HN + hh) * HD : (t * HN + hh + 1) * HD] = dkvin[t, hh]
+            dkv_ref[:, :, t, hh * HD : (hh + 1) * HD] = dkvin[t, hh]
 
     for copy in pending:
         copy.wait_send()
@@ -577,16 +582,15 @@
 
 
 def on_device(queries, image_kv, gate_logit, d_gated, media_list, media_count, image_slot):
-    kv = image_kv.reshape(2, 32, 2 * HN * HD)
     smem = pl.BlockSpec(memory_space=pltpu.SMEM)
     vmem = pl.BlockSpec(memory_space=pltpu.VMEM)
     dma = pltpu.SemaphoreType.DMA
-    gated, d_queries, d_kv = pl.pallas_call(
+    return pl.pallas_call(
         kernel,
         out_shape=(
             jax.ShapeDtypeStruct((TOK, HN * HD), BF16),
             jax.ShapeDtypeStruct((TOK, HN * HD), BF16),
-            jax.ShapeDtypeStruct((2, 32, 2 * HN * HD), BF16),
+            jax.ShapeDtypeStruct((2, 32, 2, HN * HD), BF16),
         ),
         in_specs=[smem] * 4 + [vmem] * 3,
         out_specs=(vmem,) * 3,
@@ -612,11 +616,12 @@
             pltpu.VMEM((2, 2, 3, HD, HALF), BF16),
             pltpu.VMEM((XN, MEDIA, PART, HD), BF16),
             pltpu.VMEM((XN, MEDIA, PART, HD), BF16),
-            pltpu.VMEM((2, 2, 7, 4, PART, HD), BF16),
-            pltpu.VMEM((2, 2, 7, 4, PART, HD), BF16),
+            pltpu.VMEM((2, 2, 14, 2, PART, HD), BF16),
+            pltpu.VMEM((2, 2, 14, 2, PART, HD), BF16),
             pltpu.VMEM((2, SLOTS, PART, HD), F32),
             pltpu.VMEM((2, 8, 2, 32, HD), BF16),
             pltpu.VMEM((2, HN, 2, 32, HD), BF16),
+            pltpu.VMEM((2, 32, 2 * HN * HD), BF16),
             pltpu.VMEM((8, HD), jnp.int32),
             pltpu.SMEM((8, HD), jnp.int32),
             dma,
@@ -625,16 +630,14 @@
             dma((2, 2, 3)), dma((2, 2, 3)),
             dma((4, 3)), dma((4, 3)),
             dma((2, 2, 3)), dma((2, 2, 3)),
-            dma((2, 2, 7)), dma((2, 2, 7)),
+            dma((2, 2, 14)), dma((2, 2, 14)),
             dma((2, 8)), dma((2, 8)),
         ],
         compiler_params=pltpu.CompilerParams(
             collective_id=0, has_side_effects=True, vmem_limit_bytes=60 * 1024 * 1024
         ),
         name="attend",
-    )(media_list.T, media_count, image_slot, gate_logit, queries, d_gated, kv)
-    d_image_kv = d_kv.reshape(2, 32, 2, HN * HD)
-    return gated, d_queries, d_image_kv
+    )(media_list.T, media_count, image_slot, gate_logit, queries, d_gated, image_kv)
 
 
 def solution(mesh):

time: 99.2 us -> 96 us (0.968)
  local copies, waits for them, and re-layouts: 5.62 us -> 3.61 us
  Pallas kernels: 92.8 us -> 91.5 us
    reshape x2 -> x0, local copies, waits for them, and re-layouts: 3.73 us -> none  [the longest x1 1.9 us: on_device(): d_image_kv = d_kv.reshape(2, 32, 2, HN * HD)]
    unnamed x6 -> x7, local copies, waits for them, and re-layouts: 1.89 us -> 3.61 us
    pallas_call x1, Pallas kernels: 92.8 us -> 91.5 us  [on_device(): pl.pallas_call(kernel, out_shape=(jax.ShapeDtypeStruct((TOK, HN * HD), BF...]
where the time goes in v6:
time: 96 us; the launch traced here: 95.8 us
  Pallas kernels  91.5 us (95%)
  local copies, waits for them, and re-layouts  3.61 us (4%)
    pallas_call x1, Pallas kernels, on_device(): pl.pallas_call(kernel, out_shape=(jax.ShapeDtypeStruct((TOK, HN * HD), BF...  91.5 us
    unnamed x7, local copies, waits for them, and re-layouts  3.61 us

profile of v6, /device:TPU:1, one launch (start us, length us, event | category | flops | bytes accessed | tf_op | source)
XLA Modules:
  0.0 95.8 jit_solution(12784729609810988736)
XLA Ops:
  0.6 91.5 %attend.1 = (bf16[192,1024]{1,0:T(8,128)(2,1)}, bf16[192,1024]{1,0:T(8,128)(2,1)}, bf16[2,32,2,1024]{3,2,1,0:T(2,128)(2,1)}) custom-call(s32[16,32]{1,0:T(8,128)} %bitcast.1, s32[32]{0:T(128)} %counts_ref.1, s32[64]{0:T(128)} %place_ref.1, f32[8]{0:T(128)} %gate_ref.1, bf16[192,1024]{1,0:T(8,128)(2,1)} %q_ref.1, bf16[192,1024]{1,0:T(8,128)(2,1)} %dg_ref.1, ...), custom_call_target="tpu_custom_call" | custom-call | tf_op jit(solution)/shard_map/attend/pallas_call | solution.py:588
  92.2 0.0 copy-start
  92.2 1.8 %copy.13 = bf16[192,1024]{1,0:T(8,128)(2,1)} copy(bf16[192,1024]{1,0:T(8,128)(2,1)} %get-tuple-element.6) | data formatting | bytes 786432
  94.0 0.0 copy-done
  94.0 0.0 copy-start.1
  94.0 0.7 copy.14
  94.8 0.3 copy-done.1
  95.1 0.7 copy.15
Async XLA Ops:
  92.2 1.8 %copy-start = (bf16[192,1024]{1,0:T(8,128)(2,1)S(1)}, bf16[192,1024]{1,0:T(8,128)(2,1)}, u32[]{:S(2)}) copy-start(bf16[192,1024]{1,0:T(8,128)(2,1)} %get-tuple-element.7) | copy-start | bytes 1179652
  94.0 1.1 %copy-start.1 = (bf16[2,32,2,1024]{3,2,1,0:T(2,128)(2,1)S(1)}, bf16[2,32,2,1024]{3,2,1,0:T(2,128)(2,1)}, u32[]{:S(2)}) copy-start(bf16[2,32,2,1024]{3,2,1,0:T(2,128)(2,1)} %get-tuple-element.8) | copy-start | bytes 786436

commit v7 on v6

--- a/solution.py
+++ b/solution.py
@@ -45,7 +45,7 @@
     media_ref, counts_ref, place_ref, gate_ref, q_ref, dg_ref, kv_ref,
     gated_ref, dq_ref, dkv_ref,
     kall, vall, qall, daall, dat, dap, pmat, kc, kt, vc, vt, sbuf, ot,
-    stat, statin, fac, dlt, xo, xin, gk, gv, rout, rin, sums, fin, dkvin, kvlin, inv_v, inv_ref, inv_sem,
+    stat, statin, fac, wgt, dlt, xo, xin, gk, gv, rout, rin, sums, fin, dkvin, kvlin, inv_v, inv_ref, inv_sem,
     a2a_s, a2a_r, ag_s, ag_r, xg_s, xg_r, st_s, st_r, xr_s, xr_r, rs_s, rs_r, fa_s, fa_r,
 ):
     seq = lax.axis_index("seq")
@@ -293,6 +293,8 @@
                 da_t = dat[c, :, lanes(rb)]
                 o = nn_dot(vt[c], pmat[c, :, lanes(rb)])
                 ot[c, :, lanes(rb)] = o
+                cols = pl.ds(pl.multiple_of(lax.rem(rb, 3) * RB, RB), RB)
+                xo[0, c, rb // 3, :, cols] = (o / stat[c, 1, pl.ds(rb, 1), :]).astype(BF16)
                 stat[c, 2, pl.ds(rb, 1), :] = jnp.sum(da_t.astype(F32) * o, axis=0, keepdims=True)
             return carry
 
@@ -327,9 +329,61 @@
     turn(x_opp)
     ag_end(1)
 
+    def xr_copy(t, d, i):
+        c, half = ((x_opp, d), (x_to[d], 1 - d), (x_to[d], d))[i]
+        return pltpu.make_async_remote_copy(
+            src_ref=xo.at[t, c, half], dst_ref=xin.at[t, d, i], send_sem=xr_s.at[t, d, i],
+            recv_sem=xr_r.at[t, d, i], device_id=dev(z, x_to[d], h), device_id_type=MESH,
+        )
+
+    def xr_opp(t):
+        for d in range(2):
+            xr_copy(t, d, 0).start()
+
+    def xr_near(t, d):
+        xr_copy(t, d, 1).start()
+
+    def row_of(ref, c, half):
+        return jnp.concatenate([ref[c, pl.ds(half * 3 + r, 1), :] for r in range(3)], axis=1)
+
+    def part_of(t, c, half):
+        if t == 1:
+            return xo[1, c, half].astype(F32)
+        return ot[c, :, half * HALF : (half + 1) * HALF] * row_of(fac, c, half)
+
+    def weighed(t, c, half, d, i):
+        got = xin[t, d, i].astype(F32)
+        return got * row_of(wgt.at[:, d], c, half) if t == 0 else got
+
+    def xr_add(t):
+        for d in range(2):
+            arrived(xin.at[t, d, 0], xr_r.at[t, d, 0])
+            both = part_of(t, x_to[d], d) + weighed(t, x_to[d], d, d, 0)
+            xo[t, x_to[d], d] = both.astype(BF16)
+            xr_copy(t, d, 2).start()
+
+    def xr_end(t):
+        for d in range(2):
+            for i in (1, 2):
+                arrived(xin.at[t, d, i], xr_r.at[t, d, i])
+
+    def xr_rows(t, half):
+        both = part_of(t, x, half) + xin[t, half, 2].astype(F32) + weighed(t, x, half, 1 - half, 1)
+        return both.T
+
     for c in range(XN):
         outs_of(c)
         stat_send(c, c)
+
+        @pl.when(x_opp == c)
+        def _():
+            xr_opp(0)
+
+        for d in range(2):
+
+            @pl.when(x_to[d] == c)
+            def _():
+                xr_near(0, d)
 
     def stat_wait(c):
         for k in range(1, XN):
@@ -345,14 +399,13 @@
         total = sum(a * b for a, b in zip(scales, totals))
         delta = sum(a * b for a, b in zip(scales, dots)) / total
         own = scales[0] / total
+        wgt[c, 0] = scales[1] * totals[1] / total
+        wgt[c, 1] = scales[3] * totals[3] / total
         fac[c] = own
         dlt[c] = delta * own
 
         def block(rb, carry):
-            half = rb // 3
             f = fac[c, pl.ds(rb, 1), :]
-            cols = pl.ds(pl.multiple_of(lax.rem(rb, 3) * RB, RB), RB)
-            xo[0, c, half, :, cols] = (ot[c, :, lanes(rb)] * f).astype(BF16)
             scaled = (dat[c, :, lanes(rb)].astype(F32) * f).astype(BF16)
             dat[c, :, lanes(rb)] = scaled
             dap[c, pl.ds(pl.multiple_of(rb * RB, RB), RB), :] = scaled.T
@@ -360,52 +413,14 @@
 
         lax.fori_loop(0, 6, block, 0, unroll=True)
 
-    def xr_opp(t):
-        for d in range(2):
-            send(xo.at[t, x_opp, d], xin.at[t, d, 0], xr_s.at[t, d, 0], xr_r.at[t, d, 0], dev(z, x_to[d], h))
-
-    def xr_near(t, d):
-        send(
-            xo.at[t, x_to[d], 1 - d], xin.at[t, d, 1], xr_s.at[t, d, 1], xr_r.at[t, d, 1], dev(z, x_to[d], h)
-        )
-
-    def xr_add(t):
-        for d in range(2):
-            arrived(xin.at[t, d, 0], xr_r.at[t, d, 0])
-            both = xo[t, x_to[d], d].astype(F32) + xin[t, d, 0].astype(F32)
-            xo[t, x_to[d], d] = both.astype(BF16)
-            send(
-                xo.at[t, x_to[d], d], xin.at[t, d, 2], xr_s.at[t, d, 2], xr_r.at[t, d, 2], dev(z, x_to[d], h)
-            )
-
-    def xr_end(t):
-        for d in range(2):
-            for i in (1, 2):
-                arrived(xin.at[t, d, i], xr_r.at[t, d, i])
-
-    def xr_rows(t, half):
-        both = xo[t, x, half].astype(F32) + xin[t, half, 2].astype(F32) + xin[t, 1 - half, 1].astype(F32)
-        return both.T
-
-    for c in range(XN):
-        combine(c)
-    xr_opp(0)
-    xr_near(0, 0)
-    xr_near(0, 1)
-
     def value_grads(c):
         for m in range(KEYS // MS):
             part = nn_dot(pmat[c, m * MS : (m + 1) * MS, :], dap[c])
             gv[c, m * MS // PART : (m + 1) * MS // PART] = part.astype(BF16).reshape(MS // PART, PART, HD)
 
-    def over_segments(f):
-        def one(c, carry):
-            f(c)
-            return carry
-
-        lax.fori_loop(0, XN, one, 0)
-
-    over_segments(value_grads)
+    for c in range(XN):
+        combine(c)
+        value_grads(c)
 
     def own_part(t, slot):
         out = None
@@ -512,14 +527,14 @@
 
     rs_step(1, 0)
     rs_step(1, 1)
+    xr_add(0)
     rs_prep(1)
     key_grads(x_opp)
-    key_grads(c_right)
-    rs_step(1, 2)
-    xr_add(0)
-    rs_step(1, 3)
     query_grads(x_opp)
     xr_opp(1)
+    rs_step(1, 2)
+    key_grads(c_right)
+    rs_step(1, 3)
     key_grads(c_left)
     key_grads(x)
     rs_step(0, 0)
@@ -563,6 +578,10 @@
     for copy in pending:
         copy.wait_send()
     for t in range(2):
+        for d in range(2):
+            for i in range(3):
+                xr_copy(t, d, i).wait_send()
+    for t in range(2):
         for k in range(1, HN):
             a2a_copy(t, k).wait_send()
 
@@ -611,6 +630,7 @@
             pltpu.VMEM((XN, 3, 8, RB), F32),
             pltpu.VMEM((XN - 1, XN, 3, 8, RB), F32),
             pltpu.VMEM((XN, 8, RB), F32),
+            pltpu.VMEM((XN, 2, 8, RB), F32),
             pltpu.VMEM((XN, 8, RB), F32),
             pltpu.VMEM((2, XN, 2, HD, HALF), BF16),
             pltpu.VMEM((2, 2, 3, HD, HALF), BF16),

time: 96 us -> 101 us (1.052)
  Pallas kernels: 91.5 us -> 96.5 us
    pallas_call x1, Pallas kernels: 91.5 us -> 96.5 us  [on_device(): pl.pallas_call(kernel, out_shape=(jax.ShapeDtypeStruct((TOK, HN * HD), BF...]
where the time goes in v7:
time: 101 us
  Pallas kernels  96.5 us (96%)
  local copies, waits for them, and re-layouts  3.61 us (4%)
    pallas_call x1, Pallas kernels, on_device(): pl.pallas_call(kernel, out_shape=(jax.ShapeDtypeStruct((TOK, HN * HD), BF...  96.5 us
    unnamed x7, local copies, waits for them, and re-layouts  3.61 us

profile of v7, /device:TPU:1, one launch (start us, length us, event | category | flops | bytes accessed | tf_op | source)
XLA Modules:
  0.0 100.8 jit_solution(13479473067113866574)
XLA Ops:
  0.6 96.5 %attend.1 = (bf16[192,1024]{1,0:T(8,128)(2,1)}, bf16[192,1024]{1,0:T(8,128)(2,1)}, bf16[2,32,2,1024]{3,2,1,0:T(2,128)(2,1)}) custom-call(s32[16,32]{1,0:T(8,128)} %bitcast.1, s32[32]{0:T(128)} %counts_ref.1, s32[64]{0:T(128)} %place_ref.1, f32[8]{0:T(128)} %gate_ref.1, bf16[192,1024]{1,0:T(8,128)(2,1)} %q_ref.1, bf16[192,1024]{1,0:T(8,128)(2,1)} %dg_ref.1, ...), custom_call_target="tpu_custom_call" | custom-call | tf_op jit(solution)/shard_map/attend/pallas_call | solution.py:607
  97.1 0.0 copy-start
  97.1 1.8 %copy.13 = bf16[192,1024]{1,0:T(8,128)(2,1)} copy(bf16[192,1024]{1,0:T(8,128)(2,1)} %get-tuple-element.6) | data formatting | bytes 786432
  99.0 0.0 copy-done
  99.0 0.0 copy-start.1
  99.0 0.7 copy.14
  99.7 0.3 copy-done.1
  100.0 0.7 copy.15
Async XLA Ops:
  97.1 1.8 %copy-start = (bf16[192,1024]{1,0:T(8,128)(2,1)S(1)}, bf16[192,1024]{1,0:T(8,128)(2,1)}, u32[]{:S(2)}) copy-start(bf16[192,1024]{1,0:T(8,128)(2,1)} %get-tuple-element.7) | copy-start | bytes 1179652
  99.0 1.1 %copy-start.1 = (bf16[2,32,2,1024]{3,2,1,0:T(2,128)(2,1)S(1)}, bf16[2,32,2,1024]{3,2,1,0:T(2,128)(2,1)}, u32[]{:S(2)}) copy-start(bf16[2,32,2,1024]{3,2,1,0:T(2,128)(2,1)} %get-tuple-element.8) | copy-start | bytes 786436

commit v8 on v7

--- a/solution.py
+++ b/solution.py
@@ -374,16 +374,9 @@
     for c in range(XN):
         outs_of(c)
         stat_send(c, c)
-
-        @pl.when(x_opp == c)
-        def _():
-            xr_opp(0)
-
-        for d in range(2):
-
-            @pl.when(x_to[d] == c)
-            def _():
-                xr_near(0, d)
+    xr_opp(0)
+    xr_near(0, 0)
+    xr_near(0, 1)
 
     def stat_wait(c):
         for k in range(1, XN):
@@ -527,9 +520,9 @@
 
     rs_step(1, 0)
     rs_step(1, 1)
-    xr_add(0)
     rs_prep(1)
     key_grads(x_opp)
+    xr_add(0)
     query_grads(x_opp)
     xr_opp(1)
     rs_step(1, 2)

time: 101 us -> 94.4 us (0.935)
  Pallas kernels: 96.5 us -> 90 us
    pallas_call x1, Pallas kernels: 96.5 us -> 90 us  [on_device(): pl.pallas_call(kernel, out_shape=(jax.ShapeDtypeStruct((TOK, HN * HD), BF...]
where the time goes in v8:
time: 94.4 us; the launch traced here: 94.3 us
  Pallas kernels  90 us (95%)
  local copies, waits for them, and re-layouts  3.61 us (4%)
    pallas_call x1, Pallas kernels, on_device(): pl.pallas_call(kernel, out_shape=(jax.ShapeDtypeStruct((TOK, HN * HD), BF...  90 us
    unnamed x7, local copies, waits for them, and re-layouts  3.61 us

profile of v8, /device:TPU:1, one launch (start us, length us, event | category | flops | bytes accessed | tf_op | source)
XLA Modules:
  0.0 94.3 jit_solution(11240181316794488590)
XLA Ops:
  0.6 90.0 %attend.1 = (bf16[192,1024]{1,0:T(8,128)(2,1)}, bf16[192,1024]{1,0:T(8,128)(2,1)}, bf16[2,32,2,1024]{3,2,1,0:T(2,128)(2,1)}) custom-call(s32[16,32]{1,0:T(8,128)} %bitcast.1, s32[32]{0:T(128)} %counts_ref.1, s32[64]{0:T(128)} %place_ref.1, f32[8]{0:T(128)} %gate_ref.1, bf16[192,1024]{1,0:T(8,128)(2,1)} %q_ref.1, bf16[192,1024]{1,0:T(8,128)(2,1)} %dg_ref.1, ...), custom_call_target="tpu_custom_call" | custom-call | tf_op jit(solution)/shard_map/attend/pallas_call | solution.py:600
  90.7 0.0 copy-start
  90.7 1.8 %copy.13 = bf16[192,1024]{1,0:T(8,128)(2,1)} copy(bf16[192,1024]{1,0:T(8,128)(2,1)} %get-tuple-element.6) | data formatting | bytes 786432
  92.5 0.0 copy-done
  92.5 0.0 copy-start.1
  92.5 0.7 copy.14
  93.2 0.3 copy-done.1
  93.6 0.7 copy.15
Async XLA Ops:
  90.7 1.8 %copy-start = (bf16[192,1024]{1,0:T(8,128)(2,1)S(1)}, bf16[192,1024]{1,0:T(8,128)(2,1)}, u32[]{:S(2)}) copy-start(bf16[192,1024]{1,0:T(8,128)(2,1)} %get-tuple-element.7) | copy-start | bytes 1179652
  92.5 1.1 %copy-start.1 = (bf16[2,32,2,1024]{3,2,1,0:T(2,128)(2,1)S(1)}, bf16[2,32,2,1024]{3,2,1,0:T(2,128)(2,1)}, u32[]{:S(2)}) copy-start(bf16[2,32,2,1024]{3,2,1,0:T(2,128)(2,1)} %get-tuple-element.8) | copy-start | bytes 786436

commit v9 on v8

--- a/solution.py
+++ b/solution.py
@@ -42,11 +42,12 @@
 
 
 def kernel(
-    media_ref, counts_ref, place_ref, gate_ref, q_ref, dg_ref, kv_ref,
-    gated_ref, dq_ref, dkv_ref,
+    media_ref, counts_ref, place_ref, gate_ref, q_hbm, dg_hbm, kv_hbm,
+    gated_hbm, dq_hbm, dkv_hbm,
+    q_ref, dg_ref, kv_ref, gated_ref, dq_ref, dkv_ref,
     kall, vall, qall, daall, dat, dap, pmat, kc, kt, vc, vt, sbuf, ot,
     stat, statin, fac, wgt, dlt, xo, xin, gk, gv, rout, rin, sums, fin, dkvin, kvlin, inv_v, inv_ref, inv_sem,
-    a2a_s, a2a_r, ag_s, ag_r, xg_s, xg_r, st_s, st_r, xr_s, xr_r, rs_s, rs_r, fa_s, fa_r,
+    a2a_s, a2a_r, ag_s, ag_r, xg_s, xg_r, st_s, st_r, xr_s, xr_r, rs_s, rs_r, fa_s, fa_r, in_sem, out_sem,
 ):
     seq = lax.axis_index("seq")
     h = lax.axis_index("head")
@@ -81,6 +82,17 @@
     def holder(k, jj):
         return 2 * ((2 * XN - k - 2 * jj) % XN) + jj
 
+    ins = [
+        pltpu.make_async_copy(src, dst, in_sem.at[i])
+        for i, (src, dst) in enumerate(((kv_hbm, kv_ref), (q_hbm, q_ref), (dg_hbm, dg_ref)))
+    ]
+    outs = [
+        pltpu.make_async_copy(src, dst, out_sem.at[i])
+        for i, (src, dst) in enumerate(((gated_ref, gated_hbm), (dq_ref, dq_hbm), (dkv_ref, dkv_hbm)))
+    ]
+    for copy in ins:
+        copy.start()
+
     barrier = pltpu.get_barrier_semaphore()
 
     def greet(device):
@@ -104,9 +116,11 @@
 
     for d in range(2):
         greet(dev(z_to[d], x, h))
+    ins[0].wait()
     for i in range(2):
         for t in range(2):
             kvlin[i, :, t * HN * HD : (t + 1) * HN * HD] = kv_ref[i, :, t, :]
+    ins[1].wait()
     for g in range(8):
         rows = q_ref[:, g * HD : (g + 1) * HD]
         qall[x, g // 4, (g % 4) * TOK : (g % 4 + 1) * TOK, :] = rows
@@ -114,6 +128,7 @@
     def gate_row(g):
         return jnp.tanh(jnp.full((1, HD), gate_ref[g], F32))
 
+    ins[2].wait()
     for g in range(8):
         rows = dg_ref[:, g * HD : (g + 1) * HD].astype(F32) * gate_row(g)
         daall[x, g // 4, (g % 4) * TOK : (g % 4 + 1) * TOK, :] = rows.astype(BF16)
@@ -542,16 +557,17 @@
     rs_step(0, 3)
     rs_step(1, 5)
     query_grads(x)
+    xr_add(1)
     rs_step(0, 4)
     rs_step(0, 5)
     rs_step(1, 6)
-    xr_add(1)
     xr_end(0)
     for half in range(2):
         rows = xr_rows(0, half)
         for gg in range(4):
             g = half * 4 + gg
             gated_ref[:, g * HD : (g + 1) * HD] = (rows[gg * TOK : (gg + 1) * TOK, :] * gate_row(g)).astype(BF16)
+    outs[0].start()
     rs_step(0, 6)
     rs_end(1)
     fa_start(1)
@@ -563,13 +579,17 @@
         for gg in range(4):
             g = half * 4 + gg
             dq_ref[:, g * HD : (g + 1) * HD] = rows[gg * TOK : (gg + 1) * TOK, :].astype(BF16)
+    outs[1].start()
     for t in (1, 0):
         fa_end(t)
         for hh in range(HN):
             dkv_ref[:, :, t, hh * HD : (hh + 1) * HD] = dkvin[t, hh]
+    outs[2].start()
 
     for copy in pending:
         copy.wait_send()
+    for copy in outs:
+        copy.wait()
     for t in range(2):
         for d in range(2):
             for i in range(3):
@@ -593,20 +613,37 @@
                     fa_copy(t, k, jj).wait_send()
 
 
+def hand_over(a, b, c, a_out, b_out, c_out, sem):
+    copies = [
+        pltpu.make_async_copy(src, dst, sem.at[i])
+        for i, (src, dst) in enumerate(((a, a_out), (b, b_out), (c, c_out)))
+    ]
+    for copy in copies:
+        copy.start()
+    for copy in copies:
+        copy.wait()
+
+
 def on_device(queries, image_kv, gate_logit, d_gated, media_list, media_count, image_slot):
     smem = pl.BlockSpec(memory_space=pltpu.SMEM)
-    vmem = pl.BlockSpec(memory_space=pltpu.VMEM)
+    anywhere = pl.BlockSpec(memory_space=pl.ANY)
     dma = pltpu.SemaphoreType.DMA
-    return pl.pallas_call(
+    results = pl.pallas_call(
         kernel,
         out_shape=(
             jax.ShapeDtypeStruct((TOK, HN * HD), BF16),
             jax.ShapeDtypeStruct((TOK, HN * HD), BF16),
             jax.ShapeDtypeStruct((2, 32, 2, HN * HD), BF16),
         ),
-        in_specs=[smem] * 4 + [vmem] * 3,
-        out_specs=(vmem,) * 3,
+        in_specs=[smem] * 4 + [anywhere] * 3,
+        out_specs=(anywhere,) * 3,
         scratch_shapes=[
+            pltpu.VMEM((TOK, HN * HD), BF16),
+            pltpu.VMEM((TOK, HN * HD), BF16),
+            pltpu.VMEM((2, 32, 2, HN * HD), BF16),
+            pltpu.VMEM((TOK, HN * HD), BF16),
+            pltpu.VMEM((TOK, HN * HD), BF16),
+            pltpu.VMEM((2, 32, 2, HN * HD), BF16),
             pltpu.VMEM((SLOTS, 2, 32, HD), BF16),
             pltpu.VMEM((SLOTS, 2, 32, HD), BF16),
             pltpu.VMEM((XN, 2, HALF, HD), BF16),
@@ -645,12 +682,22 @@
             dma((2, 2, 3)), dma((2, 2, 3)),
             dma((2, 2, 14)), dma((2, 2, 14)),
             dma((2, 8)), dma((2, 8)),
+            dma((3,)), dma((3,)),
         ],
         compiler_params=pltpu.CompilerParams(
             collective_id=0, has_side_effects=True, vmem_limit_bytes=60 * 1024 * 1024
         ),
         name="attend",
     )(media_list.T, media_count, image_slot, gate_logit, queries, d_gated, image_kv)
+    return pl.pallas_call(
+        hand_over,
+        out_shape=tuple(jax.ShapeDtypeStruct(one.shape, one.dtype) for one in results),
+        in_specs=[anywhere] * 3,
+        out_specs=(anywhere,) * 3,
+        scratch_shapes=[dma((3,))],
+        compiler_params=pltpu.CompilerParams(vmem_limit_bytes=60 * 1024 * 1024),
+        name="hand_over",
+    )(*results)
 
 
 def solution(mesh):

time: 94.4 us -> 123 us (1.30)
  Pallas kernels: 90 us -> 122 us
  local copies, waits for them, and re-layouts: 3.61 us -> 0 us
    pallas_call x0 -> x1, Pallas kernels: none -> 32.9 us  [on_device(): pl.pallas_call(hand_over, out_shape=tuple((jax.ShapeDtypeStruct(one.shape...]
    unnamed x7 -> x0, local copies, waits for them, and re-layouts: 3.61 us -> none
    pallas_call x1, Pallas kernels: 90 us -> 88.8 us  [on_device(): pl.pallas_call(kernel, out_shape=(jax.ShapeDtypeStruct((TOK, HN * HD), BF...]
where the time goes in v9:
time: 123 us; the launch traced here: 122 us
  Pallas kernels  122 us (99%)
    pallas_call x1, Pallas kernels, on_device(): pl.pallas_call(kernel, out_shape=(jax.ShapeDtypeStruct((TOK, HN * HD), BF...  88.8 us
    pallas_call x1, Pallas kernels, on_device(): pl.pallas_call(hand_over, out_shape=tuple((jax.ShapeDtypeStruct(one.shape...  32.9 us

profile of v9, /device:TPU:1, one launch (start us, length us, event | category | flops | bytes accessed | tf_op | source)
XLA Modules:
  0.0 122.5 jit_solution(17237422450574829702)
XLA Ops:
  0.6 88.8 %attend.1 = (bf16[192,1024]{1,0:T(8,128)(2,1)}, bf16[192,1024]{1,0:T(8,128)(2,1)}, bf16[2,32,2,1024]{3,2,1,0:T(2,128)(2,1)}) custom-call(s32[16,32]{1,0:T(8,128)} %bitcast.1, s32[32]{0:T(128)} %counts_ref.1, s32[64]{0:T(128)} %place_ref.1, f32[8]{0:T(128)} %gate_ref.1, bf16[192,1024]{1,0:T(8,128)(2,1)} %q_hbm.1, bf16[192,1024]{1,0:T(8,128)(2,1)} %dg_hbm.1, ...), custom_call_target="tpu_custom_call" | custom-call | tf_op jit(solution)/shard_map/attend/pallas_call | solution.py:631
  89.4 32.9 %hand_over.1 = (bf16[192,1024]{1,0:T(8,128)(2,1)}, bf16[192,1024]{1,0:T(8,128)(2,1)}, bf16[2,32,2,1024]{3,2,1,0:T(2,128)(2,1)}) custom-call(bf16[192,1024]{1,0:T(8,128)(2,1)} %get-tuple-element.6.a, bf16[192,1024]{1,0:T(8,128)(2,1)} %get-tuple-element.7.b, bf16[2,32,2,1024]{3,2,1,0:T(2,128)(2,1)} %get-tuple-element.8.c), custom_call_target="tpu_custom_call" | custom-call | tf_op jit(solution)/shard_map/hand_over/pallas_call | solution.py:692

commit v10 on v9

--- a/solution.py
+++ b/solution.py
@@ -613,14 +613,21 @@
                     fa_copy(t, k, jj).wait_send()
 
 
-def hand_over(a, b, c, a_out, b_out, c_out, sem):
-    copies = [
-        pltpu.make_async_copy(src, dst, sem.at[i])
-        for i, (src, dst) in enumerate(((a, a_out), (b, b_out), (c, c_out)))
+def hand_over(a, b, c, a_out, b_out, c_out, a_mid, b_mid, c_mid, in_sem, out_sem):
+    ins = [
+        pltpu.make_async_copy(src, dst, in_sem.at[i])
+        for i, (src, dst) in enumerate(((a, a_mid), (b, b_mid), (c, c_mid)))
     ]
-    for copy in copies:
+    outs = [
+        pltpu.make_async_copy(src, dst, out_sem.at[i])
+        for i, (src, dst) in enumerate(((a_mid, a_out), (b_mid, b_out), (c_mid, c_out)))
+    ]
+    for copy in ins:
         copy.start()
-    for copy in copies:
+    for one, two in zip(ins, outs):
+        one.wait()
+        two.start()
+    for copy in outs:
         copy.wait()
 
 
@@ -694,7 +701,7 @@
         out_shape=tuple(jax.ShapeDtypeStruct(one.shape, one.dtype) for one in results),
         in_specs=[anywhere] * 3,
         out_specs=(anywhere,) * 3,
-        scratch_shapes=[dma((3,))],
+        scratch_shapes=[pltpu.VMEM(one.shape, one.dtype) for one in results] + [dma((3,)), dma((3,))],
         compiler_params=pltpu.CompilerParams(vmem_limit_bytes=60 * 1024 * 1024),
         name="hand_over",
     )(*results)

time: 123 us -> 91.8 us (0.75)
  Pallas kernels: 122 us -> 90.8 us
    pallas_call x1, Pallas kernels: 32.9 us -> 2.01 us  [on_device(): pl.pallas_call(hand_over, out_shape=tuple((jax.ShapeDtypeStruct(one.shape...]
where the time goes in v10:
time: 91.8 us; the launch traced here: 91.6 us
  Pallas kernels  90.8 us (99%)
    pallas_call x1, Pallas kernels, on_device(): pl.pallas_call(kernel, out_shape=(jax.ShapeDtypeStruct((TOK, HN * HD), BF...  88.8 us
    pallas_call x1, Pallas kernels, on_device(): pl.pallas_call(hand_over, out_shape=tuple((jax.ShapeDtypeStruct(one.shape...  2.01 us

profile of v10, /device:TPU:1, one launch (start us, length us, event | category | flops | bytes accessed | tf_op | source)
XLA Modules:
  0.0 91.6 jit_solution(9493345424966316450)
XLA Ops:
  0.6 88.8 %attend.1 = (bf16[192,1024]{1,0:T(8,128)(2,1)}, bf16[192,1024]{1,0:T(8,128)(2,1)}, bf16[2,32,2,1024]{3,2,1,0:T(2,128)(2,1)}) custom-call(s32[16,32]{1,0:T(8,128)} %bitcast.1, s32[32]{0:T(128)} %counts_ref.1, s32[64]{0:T(128)} %place_ref.1, f32[8]{0:T(128)} %gate_ref.1, bf16[192,1024]{1,0:T(8,128)(2,1)} %q_hbm.1, bf16[192,1024]{1,0:T(8,128)(2,1)} %dg_hbm.1, ...), custom_call_target="tpu_custom_call" | custom-call | tf_op jit(solution)/shard_map/attend/pallas_call | solution.py:638
  89.4 2.0 %hand_over.1 = (bf16[192,1024]{1,0:T(8,128)(2,1)}, bf16[192,1024]{1,0:T(8,128)(2,1)}, bf16[2,32,2,1024]{3,2,1,0:T(2,128)(2,1)}) custom-call(bf16[192,1024]{1,0:T(8,128)(2,1)} %get-tuple-element.6.a, bf16[192,1024]{1,0:T(8,128)(2,1)} %get-tuple-element.7.b, bf16[2,32,2,1024]{3,2,1,0:T(2,128)(2,1)} %get-tuple-element.8.c), custom_call_target="tpu_custom_call" | custom-call | tf_op jit(solution)/shard_map/hand_over/pallas_call | solution.py:699
